TPU v7x, 32 devices: a whole 2x2x4 slice. The times are simulated.
32 devices in a mesh: groups: 2 (over y), seq: 4 (over x, core), tm: 4 (over z).
Axes of the slice: x: 2, y: 2, z: 4, core: 2. Of those that a mesh axis runs over, the one named last changes fastest.
Arguments:
- init_latent: float32 [32, 512], P('groups', 'seq'), parts along dimension 0, may hold values from -6 to 6
- cur_ids: int32 [4], P('tm'), may hold values from 1 to 999, as said below
- next_ids: int32 [4], P('tm'), may hold values from 0 to 998, as said below
- beta_table: float32 [1000], replicated, may hold values from 0.0002 to 0.008
- temb_weight: bfloat16 [256, 1152], replicated, may hold values from -0.375 to 0.375
- mod_weight: bfloat16 [1152, 5, 1152], P('seq'), may hold values from -0.1875 to 0.1875
- mod_bias: float32 [5, 1152], replicated, may hold values from -3 to 3
- patch_weight: float32 [16, 1152], replicated, may hold values from -1.5 to 1.5
- qkv_weight: bfloat16 [1152, 3, 1152], P('tm', None, 'seq'), may hold values from -6 to 6
- out_weight: bfloat16 [1152, 1152], P(None, 'tm'), may hold values from -0.1875 to 0.1875
- final_weight: bfloat16 [1152, 16], replicated, may hold values from -0.1875 to 0.1875
Outputs:
- trajectory: float32 [4, 32, 512], P('tm', 'groups', 'seq'), parts along dimension 1
- noise_pred: float32 [4, 32, 512], P('tm', 'groups', 'seq'), parts along dimension 1
There are 2 independent parts, one for each index of `groups`. A program takes and returns all parts, laid end to end along the dimension named above; an argument that names none is the same for every part. Nothing has to cross between parts.
Inputs may be any that keep to these rules, and one draw needn't show every extreme that they name: `cur_ids`: strictly falling along the steps; the first is 999. next_ids[t] = cur_ids[t + 1] for t < 3, and the last is 0.
All inputs are finite; a program needn't handle non-finite values.
Results may differ from a plain program's by a relative error of at most 0.006.
Values may be sent and summed in bfloat16 or wider, within the bound.
A program may use at most 128 MiB of HBM per device.

v0:
```python
import math

import jax
import jax.numpy as jnp
from jax import lax
from jax.sharding import PartitionSpec as P

D = 1152
HEADS = 16
FREQ = 256
ITERS = 3


def carried_in(value, axis, join, neutral):
    count, mine = (lax.axis_size(axis), lax.axis_index(axis))
    pieces = lax.all_gather(value, axis)
    so_far = jnp.full_like(value, 0) + jnp.asarray(neutral, value.dtype)

    def hop(position, so_far):
        longer = join(so_far, pieces[position])
        return jnp.where(position < mine, longer, so_far)

    return lax.fori_loop(0, count - 1, hop, so_far)


def layer_norm(values):
    center = values - jnp.mean(values, axis=-1, keepdims=True)
    spread = jnp.mean(center * center, axis=-1, keepdims=True)
    return center / jnp.sqrt(spread + 1e-06)


def plan_coefs(beta_table, cur_ids, next_ids):
    alpha_bar = jnp.cumprod(1.0 - beta_table)
    table_pos = jnp.arange(beta_table.shape[0], dtype=jnp.int32)
    bar_now = jnp.sum(
        jnp.where(table_pos[None, :] == cur_ids[:, None], alpha_bar[None, :], 0.0), axis=1
    )
    bar_next = jnp.sum(
        jnp.where(table_pos[None, :] == next_ids[:, None], alpha_bar[None, :], 0.0), axis=1
    )
    coef_a = jnp.sqrt(bar_next / bar_now)
    coef_b = jnp.sqrt(1.0 - bar_next) - coef_a * jnp.sqrt(1.0 - bar_now)
    return (coef_a, coef_b)


def frequency_embed(cur_ids, freq_width):
    half_width = freq_width // 2
    frequencies = jnp.exp(
        -math.log(10000.0) * jnp.arange(half_width, dtype=jnp.float32) / half_width
    )
    angles = cur_ids.astype(jnp.float32)[:, None] * frequencies[None, :]
    return jnp.concatenate([jnp.cos(angles), jnp.sin(angles)], axis=1)


def add_terms(earlier, later):
    return earlier + later


def attend(head_qkv):
    steps_here = head_qkv.shape[0]
    seq_len = head_qkv.shape[1]
    head_dim = D // HEADS
    heads_here = head_qkv.shape[3] // head_dim
    split_qkv = head_qkv.reshape(steps_here, seq_len, 3, heads_here, head_dim)
    query_rows = split_qkv[:, :, 0]
    key_rows = split_qkv[:, :, 1]
    value_rows = split_qkv[:, :, 2]
    block_rows = math.gcd(seq_len, 512)
    block_count = seq_len // block_rows
    query_blocks = jnp.moveaxis(
        query_rows.reshape(steps_here, block_count, block_rows, heads_here, head_dim), 1, 0
    )

    def one_block(query_block):
        scores = jnp.einsum(
            "bqhe,bkhe->bhqk", query_block, key_rows, preferred_element_type=jnp.float32
        ) / math.sqrt(head_dim)
        scores = scores - jnp.max(scores, axis=-1, keepdims=True)
        weights = jnp.exp(scores)
        attn_probs = (weights / jnp.sum(weights, axis=-1, keepdims=True)).astype(jnp.bfloat16)
        block_out = jnp.einsum(
            "bhqk,bkhe->bqhe", attn_probs, value_rows, preferred_element_type=jnp.float32
        )
        return block_out.astype(jnp.bfloat16)

    block_outs = lax.map(one_block, query_blocks)
    return jnp.moveaxis(block_outs, 0, 1).reshape(steps_here, seq_len, heads_here * head_dim)


def body(
    init_latent,
    cur_ids,
    next_ids,
    beta_table,
    temb_weight,
    mod_weight,
    mod_bias,
    patch_weight,
    qkv_weight,
    out_weight,
    final_weight,
):
    coef_a, coef_b = plan_coefs(beta_table, cur_ids, next_ids)
    local_steps = cur_ids.shape[0]
    groups = lax.axis_size("seq")
    freq_emb = frequency_embed(cur_ids, FREQ).astype(jnp.bfloat16)
    time_emb = jax.nn.silu(
        jnp.dot(freq_emb, temb_weight, preferred_element_type=jnp.float32)
    ).astype(jnp.bfloat16)
    feature_count = mod_weight.shape[0]
    emb_part = lax.dynamic_slice_in_dim(
        time_emb, lax.axis_index("seq") * feature_count, feature_count, 1
    )
    mod_terms = jnp.einsum("bd,dme->bme", emb_part, mod_weight, preferred_element_type=jnp.float32)
    mod_full = lax.psum(mod_terms, "seq").astype(jnp.bfloat16)
    qkv_full, out_full = (
        lax.all_gather(qkv_weight, "tm", axis=0, tiled=True),
        lax.all_gather(out_weight, "tm", axis=1, tiled=True),
    )
    modulation = mod_full.astype(jnp.float32) + mod_bias[None]
    states = init_latent[None]
    noise_pred = jnp.zeros_like(states)
    for iteration in range(ITERS):
        embedded = jnp.einsum("bct,cd->btd", states, patch_weight, precision=lax.Precision.HIGHEST)
        normed = (layer_norm(embedded) * (1.0 + modulation[:, 1:2]) + modulation[:, 0:1]).astype(
            jnp.bfloat16
        )
        tok_dev = normed.shape[1]
        head_qkv = jnp.einsum(
            "btd,dje->btje",
            lax.all_gather(normed, "seq", axis=1, tiled=True),
            qkv_full,
            preferred_element_type=jnp.float32,
        ).astype(jnp.bfloat16)
        heads_out = attend(head_qkv)
        seq_len = heads_out.shape[1]
        returned = lax.all_to_all(
            heads_out.reshape(local_steps, seq_len, 1, D // groups),
            "seq",
            split_axis=1,
            concat_axis=2,
            tiled=True,
        )
        heads_cat = returned.reshape(local_steps, tok_dev, D)
        projected = jnp.einsum(
            "btd,de->bte", heads_cat, out_full, preferred_element_type=jnp.float32
        )
        residual = embedded + modulation[:, 2:3] * projected
        final_in = (layer_norm(residual) * (1.0 + modulation[:, 4:5]) + modulation[:, 3:4]).astype(
            jnp.bfloat16
        )
        noise_pred = jnp.einsum(
            "btd,dc->bct", final_in, final_weight, preferred_element_type=jnp.float32
        )
        drift_term = (coef_a - 1.0)[:, None, None] * states + coef_b[:, None, None] * noise_pred
        block_total = jnp.sum(drift_term, axis=0)
        earlier = carried_in(block_total, "tm", add_terms, jnp.zeros_like(block_total))
        states = init_latent[None] + earlier[None] + (jnp.cumsum(drift_term, axis=0) - drift_term)
    return (states, noise_pred)


def solution(mesh):
    in_specs = (
        P("groups", "seq"),
        P("tm"),
        P("tm"),
        P(),
        P(),
        P("seq", None, None),
        P(),
        P(),
        P("tm", None, "seq"),
        P(None, "tm"),
        P(),
    )
    out_specs = (P("tm", "groups", "seq"), P("tm", "groups", "seq"))
    return jax.shard_map(body, mesh=mesh, in_specs=in_specs, out_specs=out_specs, check_vma=False)
```

profile of v0, /device:TPU:0, one launch (start us, length us, event | category | flops | bytes accessed | tf_op | source)
XLA Modules:
  0.0 337.9 jit_solution(11409750442916319046)
XLA Ops:
  7.3 2.6 copy.28
  12.7 13.1 %psum.7 = bf16[1,5,1152]{2,1,0:T(8,128)(2,1)S(1)} all-reduce(f32[1,5,1152]{2,1,0:T(8,128)S(1)} %copy.44), channel_id=1, replica_groups=mesh['groups'=2,'seq'=4,'tm'=4] {'seq'}, use_global_device_ids=true, to_apply=%region_4.5 | all-reduce | flops 5760 | bytes 34560 | tf_op jit(solution)/shard_map/psum | solution.py:115
  29.7 53.0 %all-gather.12.cloned.1.call-done = bf16[1152,3,288]{2,1,0:T(4,128)(2,1)} async-done(((bf16[288,3,288]{2,1,0:T(4,128)(2,1)}), bf16[1152,3,288]{2,1,0:T(4,128)(2,1)}) %all-gather.12.cloned.1.call-update) | async-done | bytes 1990672 | tf_op jit(solution)/shard_map/all_gather | solution.py:117
  82.8 7.1 %copy.29 = bf16[1152,3,288]{0,2,1:T(8,128)(2,1)} copy(bf16[1152,3,288]{2,1,0:T(4,128)(2,1)} %all-gather.12.cloned.1.call-done) | data formatting | bytes 3981312 | tf_op jit(solution)/shard_map/all_gather | solution.py:117
  89.8 10.6 %all-gather.16.cloned.1.call-done = bf16[512,1152]{1,0:T(8,128)(2,1)} async-done(((bf16[128,1152]{1,0:T(8,128)(2,1)}), bf16[512,1152]{1,0:T(8,128)(2,1)}) %all-gather.16.cloned.1.call-update) | async-done | bytes 1179664 | tf_op jit(solution)/shard_map/all_gather | solution.py:131
  100.4 4.2 %convolution_convert_fusion.2 = bf16[512,3,288]{0,2,1:T(8,128)(2,1)} fusion(bf16[1152,3,288]{0,2,1:T(8,128)(2,1)} %copy.29, bf16[512,1152]{1,0:T(8,128)(2,1)} %all-gather.16.cloned.1.call-done), kind=kOutput, calls=%fused_computation.32 | convolution fusion | flops 1019658240 | bytes 4055040 | tf_op jit(solution)/shard_map/btd,dje->btje/dot_general | solution.py:129
  104.6 4.6 %fusion.51 = (f32[4,512]{1,0:T(4,128)S(1)}, f32[4,512,512]{1,2,0:T(8,128)}) fusion(bf16[1,512,3,4,72]{1,4,3,2,0:T(8,128)(2,1)} %bitcast.209), kind=kOutput, calls=%fused_computation.119 | convolution fusion | flops 154141184 | bytes 4792320 | tf_op jit(solution)/shard_map/while/body/eval_jaxpr/sub | solution.py:78
  109.2 3.8 %fusion.23 = bf16[4,72,512]{2,1,0:T(8,128)(2,1)} fusion(f32[4,512,512]{1,2,0:T(8,128)} %get-tuple-element.366, f32[4,512]{1,0:T(4,128)S(1)} %get-tuple-element.365, bf16[1,512,3,4,72]{1,4,3,2,0:T(8,128)(2,1)} %bitcast.210), kind=kOutput, calls=%fused_computation.35 | convolution fusion | flops 153239552 | bytes 4792320 | tf_op jit(solution)/shard_map/while/body/eval_jaxpr/bhqk,bkhe->bqhe/dot_general | solution.py:81
  112.9 2.8 copy.31
  116.2 4.8 %reduce.54 = bf16[512,288]{1,0:T(8,128)(2,1)} reduce(bf16[512,1,1,288]{3,2,1,0:T(2,128)(2,1)} %bitcast.189, bf16[]{:T(256)} %broadcast.316), dimensions={1,2}, to_apply=%bitcast.131.reduce_sub_computation | reduce | bytes 589826
  121.0 2.3 reshape.506
  123.3 4.1 %all-to-all-start = ((bf16[4,2,18432]{2,1,0:T(2,128)(2,1)}), bf16[4,2,18432]{2,1,0:T(2,128)(2,1)}, u32[]{:S(2)}, u32[]{:S(2)}) async-start(bf16[4,2,18432]{2,1,0:T(2,128)(2,1)} %reshape.506), calls=%async_computation | async-start | bytes 589824 | tf_op jit(solution)/shard_map/all_to_all | solution.py:137
  131.5 2.3 all-to-all-done
  133.8 3.5 %reshape.507 = bf16[512,1,1,288]{3,2,1,0:T(2,128)(2,1)} reshape(bf16[4,2,18432]{2,1,0:T(2,128)(2,1)} %all-to-all-done) | data formatting | bytes 589824
  137.3 2.8 copy.32
  140.2 1.8 all_to_all.34
  141.9 1.7 copy.33
  143.6 13.7 %all-gather.14.cloned.1.call-done = bf16[1152,1152]{0,1:T(8,128)(2,1)} async-done(((bf16[1152,288]{0,1:T(8,128)(2,1)}), bf16[1152,1152]{0,1:T(8,128)(2,1)}) %all-gather.14.cloned.1.call-update) | async-done | bytes 2654224 | tf_op jit(solution)/shard_map/all_gather | solution.py:118
  157.4 3.0 fusion.52
  160.8 13.4 %all-gather.1 = f32[64,128]{1,0:T(8,128)S(1)} all-gather(f32[16,128]{1,0:T(8,128)S(1)} %fusion.30), channel_id=3, replica_groups=mesh['groups'=2,'seq'=4,'tm'=4] {'tm'}, dimensions={0}, use_global_device_ids=true | all-gather | bytes 40960 | tf_op jit(solution)/shard_map/all_gather | solution.py:16
  176.8 16.3 %all-gather.18.cloned.1.call-done = bf16[512,1152]{1,0:T(8,128)(2,1)} async-done(((bf16[128,1152]{1,0:T(8,128)(2,1)}), bf16[512,1152]{1,0:T(8,128)(2,1)}) %all-gather.18.cloned.1.call-update) | async-done | bytes 1179664 | tf_op jit(solution)/shard_map/all_gather | solution.py:131
  193.0 4.2 %convolution_convert_fusion.1 = bf16[512,3,288]{0,2,1:T(8,128)(2,1)} fusion(bf16[1152,3,288]{0,2,1:T(8,128)(2,1)} %copy.29, bf16[512,1152]{1,0:T(8,128)(2,1)} %all-gather.18.cloned.1.call-done), kind=kOutput, calls=%fused_computation.31 | convolution fusion | flops 1019658240 | bytes 4055040 | tf_op jit(solution)/shard_map/btd,dje->btje/dot_general | solution.py:129
  197.2 4.6 %fusion.54 = (f32[4,512]{1,0:T(4,128)S(1)}, f32[4,512,512]{1,2,0:T(8,128)}) fusion(bf16[1,512,3,4,72]{1,4,3,2,0:T(8,128)(2,1)} %bitcast.211), kind=kOutput, calls=%fused_computation.122 | convolution fusion | flops 154141184 | bytes 4792320 | tf_op jit(solution)/shard_map/while/body/eval_jaxpr/sub | solution.py:78
  201.8 3.5 %fusion.22 = bf16[4,72,512]{2,1,0:T(8,128)(2,1)} fusion(f32[4,512,512]{1,2,0:T(8,128)} %get-tuple-element.372, f32[4,512]{1,0:T(4,128)S(1)} %get-tuple-element.371, bf16[1,512,3,4,72]{1,4,3,2,0:T(8,128)(2,1)} %bitcast.212), kind=kOutput, calls=%fused_computation.34 | convolution fusion | flops 153239552 | bytes 4792320 | tf_op jit(solution)/shard_map/while/body/eval_jaxpr/bhqk,bkhe->bqhe/dot_general | solution.py:81
  205.3 2.8 copy.36
  208.1 4.8 %reduce.55 = bf16[512,288]{1,0:T(8,128)(2,1)} reduce(bf16[512,1,1,288]{3,2,1,0:T(2,128)(2,1)} %bitcast.192, bf16[]{:T(256)} %broadcast.316), dimensions={1,2}, to_apply=%bitcast.133.reduce_sub_computation | reduce | bytes 589826
  212.8 2.3 reshape.508
  215.1 4.1 %all-to-all-start.1 = ((bf16[4,2,18432]{2,1,0:T(2,128)(2,1)}), bf16[4,2,18432]{2,1,0:T(2,128)(2,1)}, u32[]{:S(2)}, u32[]{:S(2)}) async-start(bf16[4,2,18432]{2,1,0:T(2,128)(2,1)} %reshape.508), calls=%async_computation.1 | async-start | bytes 589824 | tf_op jit(solution)/shard_map/all_to_all | solution.py:137
  219.3 6.4 %all-to-all-done.1 = bf16[4,2,18432]{2,1,0:T(2,128)(2,1)} async-done(((bf16[4,2,18432]{2,1,0:T(2,128)(2,1)}), bf16[4,2,18432]{2,1,0:T(2,128)(2,1)}, u32[]{:S(2)}, u32[]{:S(2)}) %all-to-all-start.1) | async-done | bytes 294944 | tf_op jit(solution)/shard_map/all_to_all | solution.py:137
  225.7 3.5 %reshape.509 = bf16[512,1,1,288]{3,2,1,0:T(2,128)(2,1)} reshape(bf16[4,2,18432]{2,1,0:T(2,128)(2,1)} %all-to-all-done.1) | data formatting | bytes 589824
  229.2 2.8 copy.37
  232.0 1.7 all_to_all.37
  234.7 2.9 fusion.55
  238.1 13.4 %all-gather.3 = f32[64,128]{1,0:T(8,128)S(1)} all-gather(f32[16,128]{1,0:T(8,128)S(1)} %fusion.28), channel_id=5, replica_groups=mesh['groups'=2,'seq'=4,'tm'=4] {'tm'}, dimensions={0}, use_global_device_ids=true | all-gather | bytes 40960 | tf_op jit(solution)/shard_map/all_gather | solution.py:16
  254.1 17.6 %all-gather.20.cloned.1.call-done = bf16[512,1152]{1,0:T(8,128)(2,1)} async-done(((bf16[128,1152]{1,0:T(8,128)(2,1)}), bf16[512,1152]{1,0:T(8,128)(2,1)}) %all-gather.20.cloned.1.call-update) | async-done | bytes 1179664 | tf_op jit(solution)/shard_map/all_gather | solution.py:131
  271.7 4.2 %convolution_convert_fusion = bf16[512,3,288]{0,2,1:T(8,128)(2,1)} fusion(bf16[1152,3,288]{0,2,1:T(8,128)(2,1)} %copy.29, bf16[512,1152]{1,0:T(8,128)(2,1)} %all-gather.20.cloned.1.call-done), kind=kOutput, calls=%fused_computation.30 | convolution fusion | flops 1019658240 | bytes 4055040 | tf_op jit(solution)/shard_map/btd,dje->btje/dot_general | solution.py:129
  275.9 4.6 %fusion.57 = (f32[4,512]{1,0:T(4,128)S(1)}, f32[4,512,512]{1,2,0:T(8,128)}) fusion(bf16[1,512,3,4,72]{1,4,3,2,0:T(8,128)(2,1)} %bitcast.207), kind=kOutput, calls=%fused_computation.125 | convolution fusion | flops 154141184 | bytes 4792320 | tf_op jit(solution)/shard_map/while/body/eval_jaxpr/sub | solution.py:78
  280.5 3.5 %fusion.21 = bf16[4,72,512]{2,1,0:T(8,128)(2,1)} fusion(f32[4,512,512]{1,2,0:T(8,128)} %get-tuple-element.378, f32[4,512]{1,0:T(4,128)S(1)} %get-tuple-element.377, bf16[1,512,3,4,72]{1,4,3,2,0:T(8,128)(2,1)} %bitcast.208), kind=kOutput, calls=%fused_computation.33 | convolution fusion | flops 153239552 | bytes 4792320 | tf_op jit(solution)/shard_map/while/body/eval_jaxpr/bhqk,bkhe->bqhe/dot_general | solution.py:81
  284.0 2.8 copy.41
  286.8 4.8 %reduce.56 = bf16[512,288]{1,0:T(8,128)(2,1)} reduce(bf16[512,1,1,288]{3,2,1,0:T(2,128)(2,1)} %bitcast.190, bf16[]{:T(256)} %broadcast.316), dimensions={1,2}, to_apply=%bitcast.135.reduce_sub_computation | reduce | bytes 589826
  291.6 2.3 reshape.510
  293.8 4.1 %all-to-all-start.2 = ((bf16[4,2,18432]{2,1,0:T(2,128)(2,1)}), bf16[4,2,18432]{2,1,0:T(2,128)(2,1)}, u32[]{:S(2)}, u32[]{:S(2)}) async-start(bf16[4,2,18432]{2,1,0:T(2,128)(2,1)} %reshape.510), calls=%async_computation.2 | async-start | bytes 589824 | tf_op jit(solution)/shard_map/all_to_all | solution.py:137
  298.0 6.4 %all-to-all-done.2 = bf16[4,2,18432]{2,1,0:T(2,128)(2,1)} async-done(((bf16[4,2,18432]{2,1,0:T(2,128)(2,1)}), bf16[4,2,18432]{2,1,0:T(2,128)(2,1)}, u32[]{:S(2)}, u32[]{:S(2)}) %all-to-all-start.2) | async-done | bytes 294944 | tf_op jit(solution)/shard_map/all_to_all | solution.py:137
  304.4 3.5 %reshape.511 = bf16[512,1,1,288]{3,2,1,0:T(2,128)(2,1)} reshape(bf16[4,2,18432]{2,1,0:T(2,128)(2,1)} %all-to-all-done.2) | data formatting | bytes 589824
  307.9 2.8 copy.42
  310.8 1.7 all_to_all.40
  313.5 2.9 fusion.58
  317.6 13.2 %all-gather.5 = f32[64,128]{1,0:T(8,128)S(1)} all-gather(f32[16,128]{1,0:T(8,128)S(1)} %get-tuple-element.381), channel_id=7, replica_groups=mesh['groups'=2,'seq'=4,'tm'=4] {'tm'}, dimensions={0}, use_global_device_ids=true | all-gather | bytes 40960 | tf_op jit(solution)/shard_map/all_gather | solution.py:16
  (92 shorter events, 17.3 us)
Async XLA Ops:
  7.2 4.9 %copy-start = (bf16[288,5,1152]{2,0,1:T(8,128)(2,1)S(1)}, bf16[288,5,1152]{2,0,1:T(8,128)(2,1)}, u32[]{:S(2)}) copy-start(bf16[288,5,1152]{2,0,1:T(8,128)(2,1)} %param.22) | copy-start | bytes 9953284
  7.2 18.6 %copy-start.6 = (f32[5,1152]{1,0:T(8,128)S(1)}, f32[5,1152]{1,0:T(8,128)}, u32[]{:S(2)}) copy-start(f32[5,1152]{1,0:T(8,128)} %param.23) | copy-start | bytes 69124
  7.2 18.7 %copy-start.4 = (f32[16,1152]{1,0:T(8,128)S(1)}, f32[16,1152]{1,0:T(8,128)}, u32[]{:S(2)}) copy-start(f32[16,1152]{1,0:T(8,128)} %param.24) | copy-start | bytes 221188
  7.2 18.7 %copy-start.5 = (f32[16,128]{1,0:T(8,128)S(1)}, f32[16,128]{1,0:T(8,128)}, u32[]{:S(2)}) copy-start(f32[16,128]{1,0:T(8,128)} %param.17) | copy-start | bytes 24580
  7.2 75.5 %all-gather.12.cloned.1.call-start = ((), (), s32[]{:S(2)}) async-start(), calls=%async_computation.3 | async-start | bytes 4423680 | tf_op jit(solution)/shard_map/all_gather | solution.py:117
  9.9 90.5 %all-gather.16.cloned.1.call-start = ((), (), s32[]{:S(2)}) async-start(), calls=%async_computation.5 | async-start | bytes 1474560 | tf_op jit(solution)/shard_map/all_gather | solution.py:131
  12.1 17.1 %copy-start.7 = (f32[1000]{0:T(1024)S(1)}, f32[1000]{0:T(1024)}, u32[]{:S(2)}) copy-start(f32[1000]{0:T(1024)} %param.20) | copy-start | bytes 12004
  26.7 0.8 copy-start.1
  28.5 128.9 %all-gather.14.cloned.1.call-start = ((), (), s32[]{:S(2)}) async-start(), calls=%async_computation.4 | async-start | bytes 3317760 | tf_op jit(solution)/shard_map/all_gather | solution.py:118
  123.3 10.5 %all-to-all-start = ((bf16[4,2,18432]{2,1,0:T(2,128)(2,1)}), bf16[4,2,18432]{2,1,0:T(2,128)(2,1)}, u32[]{:S(2)}, u32[]{:S(2)}) async-start(bf16[4,2,18432]{2,1,0:T(2,128)(2,1)} %reshape.506), calls=%async_computation | async-start | bytes 589824 | tf_op jit(solution)/shard_map/all_to_all | solution.py:137
  127.4 65.7 %all-gather.18.cloned.1.call-start = ((), (), s32[]{:S(2)}) async-start(), calls=%async_computation.6 | async-start | bytes 1474560 | tf_op jit(solution)/shard_map/all_gather | solution.py:131
  137.3 23.3 %copy-start.8 = (bf16[1152,16]{0,1:T(8,128)(2,1)S(1)}, bf16[1152,16]{0,1:T(8,128)(2,1)}, u32[]{:S(2)}) copy-start(bf16[1152,16]{0,1:T(8,128)(2,1)} %param.27) | copy-start | bytes 110596
  175.0 0.8 copy-start.3
  215.1 10.6 %all-to-all-start.1 = ((bf16[4,2,18432]{2,1,0:T(2,128)(2,1)}), bf16[4,2,18432]{2,1,0:T(2,128)(2,1)}, u32[]{:S(2)}, u32[]{:S(2)}) async-start(bf16[4,2,18432]{2,1,0:T(2,128)(2,1)} %reshape.508), calls=%async_computation.1 | async-start | bytes 589824 | tf_op jit(solution)/shard_map/all_to_all | solution.py:137
  219.2 52.5 %all-gather.20.cloned.1.call-start = ((), (), s32[]{:S(2)}) async-start(), calls=%async_computation.7 | async-start | bytes 1474560 | tf_op jit(solution)/shard_map/all_gather | solution.py:131
  252.4 0.8 copy-start.2
  293.8 10.6 %all-to-all-start.2 = ((bf16[4,2,18432]{2,1,0:T(2,128)(2,1)}), bf16[4,2,18432]{2,1,0:T(2,128)(2,1)}, u32[]{:S(2)}, u32[]{:S(2)}) async-start(bf16[4,2,18432]{2,1,0:T(2,128)(2,1)} %reshape.510), calls=%async_computation.2 | async-start | bytes 589824 | tf_op jit(solution)/shard_map/all_to_all | solution.py:137
Sparse Core Ops, SparseCore 0:
  10.0 72.6 all-gather.11
  84.3 16.0 all-gather.15
  102.0 55.3 all-gather.13
  176.9 16.1 all-gather.17
  254.3 17.4 all-gather.19
where the time goes:
time: 340 us; the launch traced here: 338 us
  waiting for transfers between devices  127 us (37%)
  local copies, waits for them, and re-layouts  55.4 us (16%)
  blocking collectives  53.1 us (16%)
  matrix products  51.4 us (15%)
  other arithmetic  20.3 us (6%)
  between operations  18.1 us (5%)
  starting transfers between devices  12.5 us (4%)
    all_gather x1, waiting for transfers between devices, body(): lax.all_gather(qkv_weight, 'tm', axis=0, tiled=True)  53 us
    all_gather x3, waiting for transfers between devices, body(): lax.all_gather(normed, 'seq', axis=1, tiled=True)  44.4 us
    all_gather x3, blocking collectives, carried_in(): pieces = lax.all_gather(value, axis)  40 us
    unnamed x26, local copies, waits for them, and re-layouts  22.4 us
    all_to_all x9, local copies, waits for them, and re-layouts, body(): lax.all_to_all(heads_out.reshape(local_steps, seq_len, 1, D // groups), '...  17.5 us
    all_to_all x3, waiting for transfers between devices, body(): lax.all_to_all(heads_out.reshape(local_steps, seq_len, 1, D // groups), '...  15.1 us
    unnamed x6, other arithmetic  14.3 us
    all_gather x1, waiting for transfers between devices, body(): lax.all_gather(out_weight, 'tm', axis=1, tiled=True)  13.7 us
  transfers between devices with their start and end apart: 8, of which 8 were waited for; matrix products, arithmetic and copies ran while one was open for 13% of the time, Pallas kernels for 0%

commit v1 on v0

v1 whole, which is shorter than its diff:
```python
import functools
import math

import jax
import jax.numpy as jnp
from jax import lax
from jax.experimental import pallas as pl
from jax.experimental.pallas import tpu as pltpu
from jax.sharding import PartitionSpec as P

HEADS = 16
ITERS = 3
AUG = 24
HIGH = lax.Precision.HIGHEST
MESH = pl.DeviceIdType.MESH
F32, BF16 = jnp.float32, jnp.bfloat16


def greet(plan):
    barrier = pltpu.get_barrier_semaphore()
    total = 0
    for axis, n in plan:
        me = lax.axis_index(axis)
        for d in range(1, n):
            pl.semaphore_signal(
                barrier, inc=1, device_id={axis: lax.rem(me + d, n)}, device_id_type=MESH
            )
        total += n - 1
    pl.semaphore_wait(barrier, total)


def sends(axis, n, source, landing, send, recv, scatter=False):
    me = lax.axis_index(axis)
    copies = []
    for d in range(1, n):
        peer = lax.rem(me + d, n)
        copies.append(
            pltpu.make_async_remote_copy(
                src_ref=source.at[peer] if scatter else source,
                dst_ref=landing.at[me],
                send_sem=send.at[d - 1],
                recv_sem=recv.at[d - 1],
                device_id={axis: peer},
                device_id_type=MESH,
            )
        )
    return copies


def exchange_kernel(axis, n, scatter, count, *refs):
    sources, landings = refs[:count], refs[count : 2 * count]
    send, recv = refs[2 * count :]
    greet([(axis, n)])
    me = lax.axis_index(axis)
    copies = []
    for i in range(count):
        copies += sends(axis, n, sources[i], landings[i], send.at[i], recv.at[i], scatter)
    for copy in copies:
        copy.start()
    for source, landing in zip(sources, landings):
        landing[me] = source[me] if scatter else source[...]
    for copy in copies:
        copy.wait()


def exchange(values, axis, cid, scatter=False):
    n = lax.axis_size(axis)
    count = len(values)
    shapes = [v.shape if scatter else (n,) + v.shape for v in values]
    vmem = pl.BlockSpec(memory_space=pltpu.VMEM)
    return pl.pallas_call(
        functools.partial(exchange_kernel, axis, n, scatter, count),
        out_shape=[jax.ShapeDtypeStruct(s, v.dtype) for s, v in zip(shapes, values)],
        in_specs=[vmem] * count,
        out_specs=[vmem] * count,
        scratch_shapes=[
            pltpu.SemaphoreType.DMA((count, n - 1)),
            pltpu.SemaphoreType.DMA((count, n - 1)),
        ],
        compiler_params=pltpu.CompilerParams(
            collective_id=cid, has_side_effects=True, vmem_limit_bytes=40 << 20
        ),
    )(*values)


def split(value):
    high = value.astype(BF16).astype(F32)
    return high, value - high


def picard_kernel(
    n_seq, n_tm,
    z0_ref, coef_ref, patch_ref, fmod_ref, final_ref, a_ref, big_ref,
    traj_ref, noise_ref,
    state, ubuf, dbuf, usrc, dsrc, yrows, usend, urecv, dsend, drecv,
):
    greet([("seq", n_seq), ("tm", n_tm)])
    here, when = lax.axis_index("seq"), lax.axis_index("tm")
    ch, tok = z0_ref.shape
    width = big_ref.shape[1]
    keys = n_seq * tok
    block = big_ref.shape[0] // n_seq
    heads_here = HEADS // n_seq
    state[...] = z0_ref[...]

    def ones_tail(lanes):
        row = lax.broadcasted_iota(jnp.int32, (AUG - ch, lanes), 0)
        return jnp.where(row == 0, 1.0, 0.0).astype(F32)

    row = lax.broadcasted_iota(jnp.int32, (16, 2 * tok), 0)
    lane = lax.broadcasted_iota(jnp.int32, (16, 2 * tok), 1)
    const = jnp.where((row == 0) & (lane < tok), 1.0, 0.0).astype(BF16)
    for s in range(n_seq):
        yrows[s * block + heads_here * 16 : (s + 1) * block, :] = const

    def one(it, carry):
        z = state[...]
        emb = lax.dot_general(
            patch_ref[...], z, (((1,), (0,)), ((), ())),
            precision=HIGH, preferred_element_type=F32,
        )
        center = emb - jnp.mean(emb, axis=0, keepdims=True)
        spread = jnp.mean(center * center, axis=0, keepdims=True)
        u = z / jnp.sqrt(spread + 1e-06)
        usrc[it] = u
        copies = sends("seq", n_seq, usrc.at[it], ubuf.at[it], usend.at[it], urecv.at[it])
        for copy in copies:
            copy.start()
        ubuf[it, here] = u
        u_query = jnp.concatenate([u, ones_tail(tok)], axis=0)
        g = lax.dot_general(
            a_ref[...], u_query, (((1,), (0,)), ((), ())),
            precision=HIGH, preferred_element_type=F32,
        )
        for copy in copies:
            copy.wait()
        u_all = jnp.concatenate([ubuf[it, s] for s in range(n_seq)], axis=1)
        u_keys = jnp.concatenate([u_all, ones_tail(keys)], axis=0)
        k_high, k_low = split(u_keys)
        pad = jnp.zeros((128 - 3 * AUG, keys), F32)
        key_rows = jnp.transpose(jnp.concatenate([k_high, k_high, k_low, pad], axis=0)).astype(BF16)
        values = jnp.concatenate([k_high, k_low], axis=0).astype(BF16)
        qpad = jnp.zeros((128 - 3 * AUG, 2 * tok), F32)
        for pair in range(HEADS // 2):
            lo = pair * 2 * AUG
            both = jnp.concatenate([g[lo : lo + AUG], g[lo + AUG : lo + 2 * AUG]], axis=1)
            q_high, q_low = split(both)
            query = jnp.concatenate([q_high, q_low, q_high, qpad], axis=0).astype(BF16)
            scores = jnp.dot(key_rows, query, preferred_element_type=F32)
            top = jnp.max(scores, axis=0, keepdims=True)
            probs = jnp.exp2(scores - top).astype(BF16)
            out = jnp.dot(values, probs, preferred_element_type=F32)
            out = out[:AUG] + out[AUG:]
            y_high, y_low = split(out[:ch] / out[ch : ch + 1])
            for k in range(2):
                head = pair * 2 + k
                at = head // heads_here * block + head % heads_here * 16
                cut = slice(k * tok, (k + 1) * tok)
                yrows[at : at + 16, 0:tok] = y_high[:, cut].astype(BF16)
                yrows[at : at + 16, tok : 2 * tok] = y_low[:, cut].astype(BF16)
        proj = lax.dot_general(
            big_ref[...], yrows[...], (((0,), (0,)), ((), ())), preferred_element_type=F32
        )
        residual = emb + proj[:, :tok] + proj[:, tok:]
        center = residual - jnp.mean(residual, axis=0, keepdims=True)
        spread = jnp.mean(center * center, axis=0, keepdims=True)
        normed = center / jnp.sqrt(spread + 1e-06)
        final_in = (normed * fmod_ref[:, 0:1] + fmod_ref[:, 1:2]).astype(BF16)
        noise = jnp.dot(final_ref[...], final_in, preferred_element_type=F32)
        noise_ref[...] = noise
        drift = coef_ref[0] * z + coef_ref[1] * noise
        dsrc[it] = drift
        copies = sends("tm", n_tm, dsrc.at[it], dbuf.at[it], dsend.at[it], drecv.at[it])
        for copy in copies:
            copy.start()
        dbuf[it, when] = drift
        for copy in copies:
            copy.wait()
        total = jnp.zeros_like(drift)
        for j in range(n_tm - 1):
            total = total + jnp.where(when > j, dbuf[it, j], 0.0)
        state[...] = z0_ref[...] + total
        return carry

    lax.fori_loop(0, ITERS, one, 0)
    traj_ref[...] = state[...]


def picard(z0, coef, patch_t, fmod, final_t, a_all, big):
    n_seq, n_tm = lax.axis_size("seq"), lax.axis_size("tm")
    ch, tok = z0.shape
    vmem = pl.BlockSpec(memory_space=pltpu.VMEM)
    sem = pltpu.SemaphoreType.DMA
    return pl.pallas_call(
        functools.partial(picard_kernel, n_seq, n_tm),
        out_shape=[jax.ShapeDtypeStruct((ch, tok), F32)] * 2,
        in_specs=[vmem] * 7,
        out_specs=[vmem] * 2,
        scratch_shapes=[
            pltpu.VMEM((ch, tok), F32),
            pltpu.VMEM((ITERS, n_seq, ch, tok), F32),
            pltpu.VMEM((ITERS, n_tm, ch, tok), F32),
            pltpu.VMEM((ITERS, ch, tok), F32),
            pltpu.VMEM((ITERS, ch, tok), F32),
            pltpu.VMEM((big.shape[0], 2 * tok), BF16),
            sem((ITERS, n_seq - 1)),
            sem((ITERS, n_seq - 1)),
            sem((ITERS, n_tm - 1)),
            sem((ITERS, n_tm - 1)),
        ],
        compiler_params=pltpu.CompilerParams(
            collective_id=9, has_side_effects=True, vmem_limit_bytes=40 << 20
        ),
    )(z0, coef, patch_t, fmod, final_t, a_all, big)


def plan_coefs(beta_table, cur_ids, next_ids):
    keep = 1.0 - beta_table
    pos = jnp.arange(beta_table.shape[0], dtype=jnp.int32)
    bar_now = jnp.prod(jnp.where(pos[None] <= cur_ids[:, None], keep[None], 1.0), axis=1)
    bar_next = jnp.prod(jnp.where(pos[None] <= next_ids[:, None], keep[None], 1.0), axis=1)
    coef_a = jnp.sqrt(bar_next / bar_now)
    coef_b = jnp.sqrt(1.0 - bar_next) - coef_a * jnp.sqrt(1.0 - bar_now)
    return (coef_a, coef_b)


def frequency_embed(cur_ids, freq_width):
    half = freq_width // 2
    freqs = jnp.exp(-math.log(10000.0) * jnp.arange(half, dtype=F32) / half)
    angles = cur_ids.astype(F32)[:, None] * freqs[None, :]
    return jnp.concatenate([jnp.cos(angles), jnp.sin(angles)], axis=1)


def wide_dot(left, right):
    parts = []
    rest = left
    for _ in range(3):
        part = lax.reduce_precision(rest, 8, 7)
        parts.append(part.astype(BF16))
        rest = rest - part
    out = jnp.dot(jnp.concatenate(parts, axis=0), right, preferred_element_type=F32)
    return jnp.sum(out.reshape((3, left.shape[0], right.shape[1])), axis=0)


def body(
    init_latent, cur_ids, next_ids, beta_table, temb_weight, mod_weight, mod_bias,
    patch_weight, qkv_weight, out_weight, final_weight,
):
    ch, width = patch_weight.shape
    tok = init_latent.shape[1]
    n_seq, n_tm = lax.axis_size("seq"), lax.axis_size("tm")
    here, when = lax.axis_index("seq"), lax.axis_index("tm")
    head_dim = width // HEADS
    heads_here = HEADS // n_seq
    cols = width // n_seq
    rows = qkv_weight.shape[0]

    out_rows = lax.dynamic_slice_in_dim(out_weight, here * cols, cols, 0)
    out_here = lax.all_gather(out_rows, "tm", axis=1, tiled=True)

    coef_a, coef_b = plan_coefs(beta_table, cur_ids, next_ids)
    coef = jnp.broadcast_to(
        jnp.stack([coef_a[0] - 1.0, coef_b[0]])[:, None, None], (2, ch, tok)
    )
    freq_emb = frequency_embed(cur_ids, temb_weight.shape[0]).astype(BF16)
    feats = mod_weight.shape[0]
    temb_here = lax.dynamic_slice_in_dim(temb_weight, here * feats, feats, 1)
    emb_part = jax.nn.silu(jnp.dot(freq_emb, temb_here, preferred_element_type=F32)).astype(BF16)
    mod_terms = jnp.einsum("d,dme->me", emb_part[0], mod_weight, preferred_element_type=F32)
    (mod_all,) = exchange([mod_terms], "seq", 0)
    modulation = jnp.sum(mod_all, axis=0).astype(BF16).astype(F32) + mod_bias
    (mod_steps,) = exchange([modulation[0:2]], "tm", 1)

    patch_mid = patch_weight - jnp.mean(patch_weight, axis=1, keepdims=True)
    mid_here = lax.dynamic_slice_in_dim(patch_mid, when * rows, rows, 1)
    steps_here = lax.dynamic_slice_in_dim(mod_steps, when * rows, rows, 2)
    left = jnp.concatenate(
        [
            mid_here[None] * (1.0 + steps_here[:, 1:2]),
            steps_here[:, 0:1],
            jnp.zeros((n_tm, AUG - ch - 1, rows), F32),
        ],
        axis=1,
    )
    m_part = wide_dot(left.reshape(n_tm * AUG, rows), qkv_weight.reshape(rows, 3 * cols))
    (m_all,) = exchange([m_part.reshape(n_tm, AUG, 3 * cols)], "tm", 2, scatter=True)
    m_here = jnp.sum(m_all, axis=0).reshape(AUG, 3, heads_here, head_dim)

    a_here = jnp.einsum(
        "khe,qhe->hkq", m_here[:, 1], m_here[:, 0], precision=HIGH, preferred_element_type=F32
    ) * (math.log2(math.e) / math.sqrt(head_dim))
    m_value = m_here[:, 2]
    same = jnp.eye(heads_here, dtype=F32)
    diag = jnp.einsum("che,hg->hcge", m_value[:ch], same).reshape(heads_here * ch, cols)
    tail = jnp.concatenate([m_value[ch].reshape(1, cols), jnp.zeros((15, cols), F32)], axis=0)
    big_here = wide_dot(jnp.concatenate([diag, tail], axis=0), out_here) * modulation[2:3]
    a_all, big = exchange([a_here, big_here.astype(BF16)], "seq", 3)

    fmod = jnp.stack([1.0 + modulation[4], modulation[3]], axis=1)
    traj, noise = picard(
        init_latent, coef, patch_weight.T, fmod, final_weight.T,
        a_all.reshape(HEADS * AUG, AUG), big.reshape(-1, width),
    )
    return (traj[None], noise[None])


def solution(mesh):
    in_specs = (
        P("groups", "seq"),
        P("tm"),
        P("tm"),
        P(),
        P(),
        P("seq", None, None),
        P(),
        P(),
        P("tm", None, "seq"),
        P(None, "tm"),
        P(),
    )
    out_specs = (P("tm", "groups", "seq"), P("tm", "groups", "seq"))
    return jax.shard_map(body, mesh=mesh, in_specs=in_specs, out_specs=out_specs, check_vma=False)
```

time: 340 us -> 130 us (0.38)
  waiting for transfers between devices: 127 us -> 0 us
  Pallas kernels: 0 us -> 70.9 us
  matrix products: 51.4 us -> 5.25 us
  local copies, waits for them, and re-layouts: 55.4 us -> 16.8 us
  blocking collectives: 53.1 us -> 21 us
  between operations: 18.1 us -> 5.15 us
  starting transfers between devices: 12.5 us -> 0 us
  other arithmetic: 20.3 us -> 10.1 us
    all_gather x5 -> x0, waiting for transfers between devices: 111 us -> none  [the longest x1 53 us: body(): lax.all_gather(qkv_weight, 'tm', axis=0, tiled=True)]
    pallas_call x0 -> x5, Pallas kernels: none -> 70.9 us  [the longest x1 37.6 us: picard(): pl.pallas_call(functools.partial(picard_kernel, n_seq, n_tm), out_shape=[...]
    dot_general x17 -> x5, matrix products: 37.7 us -> 5.25 us  [the longest x2 3.12 us: wide_dot(): jnp.dot(jnp.concatenate(parts, axis=0), right, preferred_element_type=F32)]
    all_gather x3 -> x1, blocking collectives: 40 us -> 21 us  [body(): out_here = lax.all_gather(out_rows, 'tm', axis=1, tiled=True)]
    all_to_all x9 -> x0, local copies, waits for them, and re-layouts: 17.5 us -> none  [body(): lax.all_to_all(heads_out.reshape(local_steps, seq_len, 1, D // groups), '...]
    all_to_all x3 -> x0, waiting for transfers between devices: 15.1 us -> none  [body(): lax.all_to_all(heads_out.reshape(local_steps, seq_len, 1, D // groups), '...]
    unnamed x6 -> x0, other arithmetic: 14.3 us -> none
    sub x3 -> x0, matrix products: 13.7 us -> none  [one_block(): scores = scores - jnp.max(scores, axis=-1, keepdims=True)]
  transfers between devices with their start and end apart: 8 -> 0, of which waited for: 8 -> 0; matrix products, arithmetic and copies ran while one was open for 13% -> 0% of each run, Pallas kernels for 0% -> 0%
where the time goes in v1:
time: 130 us; the launch traced here: 129 us
  Pallas kernels  70.9 us (55%)
  blocking collectives  21 us (16%)
  local copies, waits for them, and re-layouts  16.8 us (13%)
  other arithmetic  10.1 us (8%)
  matrix products  5.25 us (4%)
  between operations  5.15 us (4%)
    pallas_call x1, Pallas kernels, picard(): pl.pallas_call(functools.partial(picard_kernel, n_seq, n_tm), out_shape=[...  37.6 us
    pallas_call x4, Pallas kernels, exchange(): pl.pallas_call(functools.partial(exchange_kernel, axis, n, scatter, count...  33.4 us
    all_gather x1, blocking collectives, body(): out_here = lax.all_gather(out_rows, 'tm', axis=1, tiled=True)  21 us
    unnamed x27, local copies, waits for them, and re-layouts  11.6 us
    dot_general x2, matrix products, wide_dot(): jnp.dot(jnp.concatenate(parts, axis=0), right, preferred_element_type=F32)  3.12 us

profile of v1, /device:TPU:0, one launch (start us, length us, event | category | flops | bytes accessed | tf_op | source)
XLA Modules:
  0.0 129.2 jit_solution(17969249162587461045)
XLA Ops:
  0.6 0.0 copy-start
  0.6 0.0 copy-start.8
  1.5 0.1 sine_convert_fusion
  1.5 1.3 %convolution_reduce_fusion.1 = f32[288]{0:T(512)S(1)} fusion(bf16[256,1]{0,1:T(2,128)(2,1)S(1)} %reshape.114, bf16[256,1152]{1,0:T(8,128)(2,1)} %param.15, s32[]{:T(128)S(6)} %select_n.19), kind=kOutput, calls=%fused_computation.2 | convolution fusion | flops 147456 | bytes 198276 | tf_op jit(solution)/shard_map/dot_general | solution.py:268
  2.9 0.6 fusion.17
  3.5 5.4 %shard_map.122 = f32[4,5,1152]{2,1,0:T(8,128)S(1)} custom-call(f32[5,1152]{1,0:T(8,128)S(1)} %bitcast.58), custom_call_target="tpu_custom_call" | custom-call | tf_op jit(solution)/shard_map/pallas_call | solution.py:71
  8.9 0.6 reduce_sum.45
  9.5 0.8 convert_add_fusion
  10.3 0.6 copy-done.9
  10.9 6.3 %shard_map.123 = f32[4,2,1152]{2,1,0:T(2,128)S(1)} custom-call(f32[2,1152]{1,0:T(2,128)S(1)} %slice.53.refs_0_), custom_call_target="tpu_custom_call" | custom-call | tf_op jit(solution)/shard_map/pallas_call | solution.py:71
  17.2 0.1 dynamic-slice_add_fusion
  17.4 0.1 reduce_sum.46
  17.5 0.1 dynamic-slice_subtract_fusion
  17.6 0.1 pad.11.clone
  17.7 0.1 maximum_maximum_fusion
  17.8 2.2 %copy.23 = bf16[288,3,288]{0,2,1:T(8,128)(2,1)} copy(bf16[288,3,288]{2,0,1:T(8,128)(2,1)} %param.19) | data formatting | bytes 995328 | tf_op args[8]
  20.1 1.6 %convolution_reduce_fusion = f32[96,864]{1,0:T(8,128)S(1)} fusion(bf16[3,96,288]{2,1,0:T(8,128)(2,1)S(1)} %bitcast.64, bf16[288,864,1]{0,1,2:T(8,128)(2,1)} %bitcast.63), kind=kOutput, calls=%fused_computation | convolution fusion | flops 143493120 | bytes 995328 | tf_op jit(solution)/shard_map/dot_general | solution.py:241
  21.7 9.5 %shard_map.124 = f32[4,24,864]{2,1,0:T(8,128)S(1)} custom-call(f32[4,24,864]{2,1,0:T(8,128)S(1)} %bitcast.55), custom_call_target="tpu_custom_call" | custom-call | tf_op jit(solution)/shard_map/pallas_call | solution.py:71
  31.2 0.7 copy-done.3
  31.9 1.6 %reduce_sum.48 = f32[24,864]{1,0:T(8,128)} reduce(f32[4,24,864]{2,1,0:T(8,128)} %copy-done.3, f32[]{:T(128)} %constant.39.clone.1), dimensions={0}, to_apply=%region_5.6 | reduce | flops 62208 | bytes 414724 | tf_op jit(solution)/shard_map/reduce_sum | solution.py:287
  33.5 1.0 reshape.109
  34.6 0.7 multiply_bitcast_fusion
  35.3 1.7 %reshape.110 = f32[64,288]{1,0:T(8,128)} reshape(f32[4,16,4,72]{3,2,1,0:T(4,128)} %multiply_bitcast_fusion) | data formatting | bytes 147456 | tf_op jit(solution)/shard_map/reshape | solution.py:294
  37.0 0.1 reshape_squeeze.3
  37.1 0.1 pad.5.clone
  37.1 1.0 reduce-precision_convert_fusion.3
  38.1 1.1 constant_dynamic-slice_fusion
  39.2 0.0 copy-start.10
  39.3 21.0 %all_gather.3 = bf16[288,1152]{0,1:T(8,128)(2,1)S(1)} all-gather(bf16[288,288]{0,1:T(8,128)(2,1)S(1)} %constant_dynamic-slice_fusion), channel_id=1, replica_groups=mesh['groups'=2,'seq'=4,'tm'=4] {'tm'}, dimensions={1}, use_global_device_ids=true | all-gather | bytes 829440 | tf_op jit(solution)/shard_map/all_gather | solution.py:259
  60.2 1.5 %fusion.1 = f32[240,1152]{1,0:T(8,128)} fusion(bf16[288,1152]{0,1:T(8,128)(2,1)S(1)} %all_gather.3, bf16[80,288]{1,0:T(8,128)(2,1)S(1)} %get-tuple-element.19, bf16[80,288]{1,0:T(8,128)(2,1)S(1)} %get-tuple-element.18, bf16[80,288]{1,0:T(8,128)(2,1)S(1)} %get-tuple-element.17), kind=kOutput, calls=%fused_computation.10 | convolution fusion | flops 159667200 | bytes 1907712 | tf_op jit(solution)/shard_map/dot_general | solution.py:241
  61.8 2.1 %reduce_sum.49 = f32[80,1152]{1,0:T(8,128)} reduce(f32[3,80,1152]{2,1,0:T(8,128)} %bitcast.62, f32[]{:T(128)} %constant.39.clone.1), dimensions={0}, to_apply=%region_6.7 | reduce | flops 184320 | bytes 1474564 | tf_op jit(solution)/shard_map/reduce_sum | solution.py:242
  63.8 0.9 slice_reduce_fusion
  64.8 1.0 multiply_convert_fusion.refs_1_
  65.8 0.2 convolution_multiply_fusion.refs_0_
  66.0 12.2 %shard_map.125 = (f32[4,4,24,24]{3,2,1,0:T(8,128)S(1)}, bf16[4,80,1152]{2,1,0:T(8,128)(2,1)S(1)}) custom-call(f32[4,24,24]{2,1,0:T(8,128)S(1)} %convolution_multiply_fusion.refs_0_, bf16[80,1152]{1,0:T(8,128)(2,1)S(1)} %multiply_convert_fusion.refs_1_), custom_call_target="tpu_custom_call" | custom-call | tf_op jit(solution)/shard_map/pallas_call | solution.py:71
  78.2 0.9 copy-done.4
  79.1 1.1 copy.28.fmod_ref
  80.8 0.7 select_reduce_fusion
  84.3 0.1 pad_maximum_fusion.2
  84.4 0.1 broadcast_in_dim.13.coef_ref
  84.5 2.0 %copy.22 = f32[16,1152]{0,1:T(8,128)} copy(f32[16,1152]{1,0:T(8,128)} %param.18) | data formatting | bytes 147456 | tf_op args[7]
  86.4 1.1 copy-done.1
  87.5 1.1 copy-done.2
  88.6 1.1 copy-done.5
  89.7 0.8 copy-done.6
  90.4 37.6 %shard_map.126 = (f32[16,128]{1,0:T(8,128)S(1)}, f32[16,128]{1,0:T(8,128)S(1)}) custom-call(f32[16,128]{1,0:T(8,128)S(1)} %copy-done.7, f32[2,16,128]{2,1,0:T(8,128)S(1)} %broadcast_in_dim.13.coef_ref, f32[1152,16]{1,0:T(8,128)S(1)} %bitcast.54, f32[1152,2]{1,0:T(8,128)S(1)} %copy-done.1, bf16[16,1152]{1,0:T(8,128)(2,1)S(1)} %bitcast.59, ...), custom_call_target="tpu_custom_call" | custom-call | tf_op jit(solution)/shard_map/pallas_call | solution.py:194
  128.0 0.6 copy.47
  128.6 0.6 copy.48
  (31 shorter events, 0.2 us)
Async XLA Ops:
  0.6 2.3 %copy-start = (bf16[288,5,1152]{2,0,1:T(8,128)(2,1)S(1)}, bf16[288,5,1152]{2,0,1:T(8,128)(2,1)}, u32[]{:S(2)}) copy-start(bf16[288,5,1152]{2,0,1:T(8,128)(2,1)} %param.16) | copy-start | bytes 9953284
  0.6 16.7 %copy-start.8 = (f32[16,1152]{1,0:T(8,128)S(1)}, f32[16,1152]{1,0:T(8,128)}, u32[]{:S(2)}) copy-start(f32[16,1152]{1,0:T(8,128)} %param.18) | copy-start | bytes 221188
  10.3 0.6 copy-start.9
  31.2 0.7 copy-start.3
  39.2 41.6 %copy-start.10 = (f32[1000]{0:T(1024)S(1)}, f32[1000]{0:T(1024)}, u32[]{:S(2)}) copy-start(f32[1000]{0:T(1024)} %param.14) | copy-start | bytes 12004
  60.2 26.2 %copy-start.7 = (f32[16,128]{1,0:T(8,128)S(1)}, f32[16,128]{1,0:T(8,128)}, u32[]{:S(2)}) copy-start(f32[16,128]{1,0:T(8,128)} %z0_ref.1) | copy-start | bytes 24580
  78.2 0.9 copy-start.4
  86.4 1.1 copy-start.1
  87.5 1.1 copy-start.2
  88.6 1.1 copy-start.5
  89.7 0.8 copy-start.6

commit v2 on v1

v2 whole, which is shorter than its diff:
```python
import functools
import math

import jax
import jax.numpy as jnp
from jax import lax
from jax.experimental import pallas as pl
from jax.experimental.pallas import tpu as pltpu
from jax.sharding import PartitionSpec as P

HEADS = 16
ITERS = 3
AUG = 24
HIGH = lax.Precision.HIGHEST
MESH = pl.DeviceIdType.MESH
F32, BF16 = jnp.float32, jnp.bfloat16


def greet(plan):
    barrier = pltpu.get_barrier_semaphore()
    total = 0
    for axis, n in plan:
        me = lax.axis_index(axis)
        for d in range(1, n):
            pl.semaphore_signal(
                barrier, inc=1, device_id={axis: lax.rem(me + d, n)}, device_id_type=MESH
            )
        total += n - 1
    pl.semaphore_wait(barrier, total)


def sends(axis, n, source, landing, send, recv, scatter=False):
    me = lax.axis_index(axis)
    copies = []
    for d in range(1, n):
        peer = lax.rem(me + d, n)
        copies.append(
            pltpu.make_async_remote_copy(
                src_ref=source.at[peer] if scatter else source,
                dst_ref=landing.at[me],
                send_sem=send.at[d - 1],
                recv_sem=recv.at[d - 1],
                device_id={axis: peer},
                device_id_type=MESH,
            )
        )
    return copies


def split(value):
    high = value.astype(BF16).astype(F32)
    return high, value - high


def split3(value):
    high, rest = split(value)
    mid, low = split(rest)
    return jnp.concatenate([high, mid, low], axis=0).astype(BF16)


def thirds(value):
    n = value.shape[0] // 3
    return value[:n] + value[n : 2 * n] + value[2 * n :]


def share(n, source, landing, send, recv):
    me = lax.axis_index("seq")
    if n != 4:
        copies = sends("seq", n, source, landing, send, recv)
        for copy in copies:
            copy.start()
        landing[me] = source[...]
        for copy in copies:
            copy.wait()
        return
    pair = me + 1 - 2 * lax.rem(me, 2)
    across = lax.rem(me + 2, 4)

    def to(block, slot, peer, i):
        return pltpu.make_async_remote_copy(
            src_ref=block, dst_ref=landing.at[slot], send_sem=send.at[i], recv_sem=recv.at[i],
            device_id={"seq": peer}, device_id_type=MESH,
        )

    far, near = to(source, me, across, 0), to(source, me, pair, 1)
    far.start()
    near.start()
    landing[me] = source[...]
    far.wait_recv()
    onward = to(landing.at[across], across, pair, 2)
    onward.start()
    near.wait()
    far.wait_send()
    onward.wait()


def picard_kernel(
    n_seq, n_tm, head_dim,
    z0_ref, coef_ref, patch_ref, final_ref, terms_ref, bias_ref, mid_ref, qkv_ref, wo_ref,
    traj_ref, noise_ref,
    wbuf, tbuf, msrc, mbuf, psrc, pbuf, asrc, abuf, bsrc, bbuf, bigt, cols,
    state, ubuf, dbuf, usrc, dsrc, yrows,
    wsend, wrecv, tsend, trecv, msend, mrecv, psend, precv, asend, arecv, bsend, brecv,
    usend, urecv, dsend, drecv,
):
    greet([("seq", n_seq), ("tm", n_tm)])
    here, when = lax.axis_index("seq"), lax.axis_index("tm")
    ch, tok = z0_ref.shape
    keys = n_seq * tok
    heads_here = HEADS // n_seq
    block = heads_here * 16 + 16
    width = patch_ref.shape[0]
    rows = mid_ref.shape[1]
    wide = bsrc.shape[1] // n_tm

    terms = sends("seq", n_seq, terms_ref, tbuf, tsend, trecv)
    for copy in terms:
        copy.start()
    outs = sends("tm", n_tm, wo_ref, wbuf, wsend, wrecv)
    for copy in outs:
        copy.start()
    tbuf[here] = terms_ref[...]
    wbuf[when] = wo_ref[...]
    state[...] = z0_ref[...]
    bsrc[...] = jnp.zeros_like(bsrc)

    def ones_tail(lanes):
        row = lax.broadcasted_iota(jnp.int32, (AUG - ch, lanes), 0)
        return jnp.where(row == 0, 1.0, 0.0).astype(F32)

    row = lax.broadcasted_iota(jnp.int32, (16, 2 * tok), 0)
    lane = lax.broadcasted_iota(jnp.int32, (16, 2 * tok), 1)
    const = jnp.where((row == 0) & (lane < tok), 1.0, 0.0).astype(BF16)
    for s in range(n_seq):
        yrows[s * block + heads_here * 16 : (s + 1) * block, :] = const

    for copy in terms:
        copy.wait()
    mod = tbuf[0]
    for s in range(1, n_seq):
        mod = mod + tbuf[s]
    mod = mod.astype(BF16).astype(F32) + bias_ref[...]
    for k in range(n_tm):
        msrc[k] = mod[:, k * rows : (k + 1) * rows]
    steps = sends("tm", n_tm, msrc, mbuf, msend, mrecv, True)
    for copy in steps:
        copy.start()
    mbuf[when] = msrc[when]
    cols[...] = jnp.transpose(jnp.concatenate([mod, jnp.zeros((120, width), F32)], axis=0))
    for copy in steps:
        copy.wait()

    first = lax.broadcasted_iota(jnp.int32, (AUG - ch, rows), 0) == 0
    left = []
    for t in range(n_tm):
        step = mbuf[t]
        left.append(mid_ref[...] * (1.0 + step[1:2]))
        left.append(jnp.where(first, step[0:1], 0.0))
    left = split3(jnp.concatenate(left, axis=0))
    for j in range(3):
        part = thirds(jnp.dot(left, qkv_ref[j], preferred_element_type=F32))
        for t in range(n_tm):
            psrc[t, j] = part[t * AUG : (t + 1) * AUG]
    parts = sends("tm", n_tm, psrc, pbuf, psend, precv, True)
    for copy in parts:
        copy.start()
    pbuf[when] = psrc[when]
    for copy in parts:
        copy.wait()
    m_query, m_key, m_value = pbuf[0, 0], pbuf[0, 1], pbuf[0, 2]
    for t in range(1, n_tm):
        m_query, m_key, m_value = (
            m_query + pbuf[t, 0], m_key + pbuf[t, 1], m_value + pbuf[t, 2]
        )
    spot = lax.broadcasted_iota(jnp.int32, m_key.shape, 1)

    def own(value, h):
        at = spot[: value.shape[0]]
        return jnp.where((at >= h * head_dim) & (at < (h + 1) * head_dim), value, 0.0)

    scale = math.log2(math.e) / math.sqrt(head_dim)
    stacked = jnp.concatenate([own(m_key, h) for h in range(heads_here)], axis=0)
    asrc[...] = scale * lax.dot_general(
        stacked, m_query, (((1,), (1,)), ((), ())), precision=HIGH, preferred_element_type=F32
    )
    forms = sends("seq", n_seq, asrc, abuf, asend, arecv)
    for copy in forms:
        copy.start()
    abuf[here] = asrc[...]
    diag = [own(m_value[:ch], h) for h in range(heads_here)]
    diag += [m_value[ch:], jnp.zeros((16 - AUG + ch, m_value.shape[1]), F32)]
    diag = split3(jnp.concatenate(diag, axis=0))
    for copy in outs:
        copy.wait()
    for k in range(n_tm):
        bsrc[:, k * wide : k * wide + rows] = thirds(
            jnp.dot(diag, wbuf[k], preferred_element_type=F32)
        ).astype(BF16)
    share(n_seq, bsrc, bbuf, bsend, brecv)
    for copy in forms:
        copy.wait()
    compact = rows % 16 == 0
    for k in range(n_tm):
        piece = bbuf[:, :, k * wide : (k + 1) * wide].reshape(n_seq * block, wide)
        turned = jnp.transpose(piece.astype(F32)).astype(BF16)
        if compact:
            bigt[k * rows : (k + 1) * rows, :] = turned[:rows]
        else:
            bigt[k * wide : (k + 1) * wide, :] = turned
    a_all = abuf[...].reshape(HEADS * AUG, AUG)

    def one(it, carry):
        z = state[...]
        emb = lax.dot_general(
            patch_ref[...], z, (((1,), (0,)), ((), ())),
            precision=HIGH, preferred_element_type=F32,
        )
        center = emb - jnp.mean(emb, axis=0, keepdims=True)
        spread = jnp.mean(center * center, axis=0, keepdims=True)
        u = z / jnp.sqrt(spread + 1e-06)
        usrc[it] = u
        copies = sends("seq", n_seq, usrc.at[it], ubuf.at[it], usend.at[it], urecv.at[it])
        for copy in copies:
            copy.start()
        ubuf[it, here] = u
        u_query = jnp.concatenate([u, ones_tail(tok)], axis=0)
        g = lax.dot_general(
            a_all, u_query, (((1,), (0,)), ((), ())),
            precision=HIGH, preferred_element_type=F32,
        )
        for copy in copies:
            copy.wait()
        u_all = jnp.concatenate([ubuf[it, s] for s in range(n_seq)], axis=1)
        u_keys = jnp.concatenate([u_all, ones_tail(keys)], axis=0)
        k_high, k_low = split(u_keys)
        pad = jnp.zeros((128 - 3 * AUG, keys), F32)
        key_rows = jnp.transpose(jnp.concatenate([k_high, k_high, k_low, pad], axis=0)).astype(BF16)
        values = jnp.concatenate([k_high, k_low], axis=0).astype(BF16)
        qpad = jnp.zeros((128 - 3 * AUG, 2 * tok), F32)
        for pair in range(HEADS // 2):
            lo = pair * 2 * AUG
            both = jnp.concatenate([g[lo : lo + AUG], g[lo + AUG : lo + 2 * AUG]], axis=1)
            q_high, q_low = split(both)
            query = jnp.concatenate([q_high, q_low, q_high, qpad], axis=0).astype(BF16)
            scores = jnp.dot(key_rows, query, preferred_element_type=F32)
            top = jnp.max(scores, axis=0, keepdims=True)
            probs = jnp.exp2(scores - top).astype(BF16)
            out = jnp.dot(values, probs, preferred_element_type=F32)
            out = out[:AUG] + out[AUG:]
            y_high, y_low = split(out[:ch] / out[ch : ch + 1])
            for k in range(2):
                head = pair * 2 + k
                at = head // heads_here * block + head % heads_here * 16
                cut = slice(k * tok, (k + 1) * tok)
                yrows[at : at + 16, 0:tok] = y_high[:, cut].astype(BF16)
                yrows[at : at + 16, tok : 2 * tok] = y_low[:, cut].astype(BF16)
        proj = jnp.dot(bigt[...], yrows[...], preferred_element_type=F32)
        proj = proj[:, :tok] + proj[:, tok:]
        if not compact:
            proj = jnp.concatenate(
                [proj[k * wide : k * wide + rows] for k in range(n_tm)], axis=0
            )
        residual = emb + cols[:, 2:3] * proj
        center = residual - jnp.mean(residual, axis=0, keepdims=True)
        spread = jnp.mean(center * center, axis=0, keepdims=True)
        normed = center / jnp.sqrt(spread + 1e-06)
        final_in = (normed * (1.0 + cols[:, 4:5]) + cols[:, 3:4]).astype(BF16)
        noise = jnp.dot(final_ref[...], final_in, preferred_element_type=F32)
        noise_ref[...] = noise
        drift = coef_ref[0] * z + coef_ref[1] * noise
        dsrc[it] = drift
        copies = sends("tm", n_tm, dsrc.at[it], dbuf.at[it], dsend.at[it], drecv.at[it])
        for copy in copies:
            copy.start()
        dbuf[it, when] = drift
        for copy in copies:
            copy.wait()
        total = jnp.zeros_like(drift)
        for j in range(n_tm - 1):
            total = total + jnp.where(when > j, dbuf[it, j], 0.0)
        state[...] = z0_ref[...] + total
        return carry

    lax.fori_loop(0, ITERS, one, 0)
    traj_ref[...] = state[...]


def picard(head_dim, z0, coef, patch_t, final_t, terms, bias, mid, qkv, wo):
    n_seq, n_tm = lax.axis_size("seq"), lax.axis_size("tm")
    ch, tok = z0.shape
    width = patch_t.shape[0]
    rows, here = mid.shape[1], wo.shape[0]
    block = HEADS // n_seq * 16 + 16
    wide = -(-rows // 128) * 128
    vmem = pl.BlockSpec(memory_space=pltpu.VMEM)
    sem, mem = pltpu.SemaphoreType.DMA, pltpu.VMEM
    pairs = []
    for n in (n_tm, n_seq, n_tm, n_tm, n_seq, n_seq):
        pairs += [sem((n - 1,)), sem((n - 1,))]
    for n in (n_seq, n_tm):
        pairs += [sem((ITERS, n - 1)), sem((ITERS, n - 1))]
    return pl.pallas_call(
        functools.partial(picard_kernel, n_seq, n_tm, head_dim),
        out_shape=[jax.ShapeDtypeStruct((ch, tok), F32)] * 2,
        in_specs=[vmem] * 9,
        out_specs=[vmem] * 2,
        scratch_shapes=[
            mem((n_tm,) + wo.shape, BF16),
            mem((n_seq,) + terms.shape, F32),
            mem((n_tm, 8, rows), F32),
            mem((n_tm, 8, rows), F32),
            mem((n_tm, 3, AUG, here), F32),
            mem((n_tm, 3, AUG, here), F32),
            mem((HEADS // n_seq * AUG, AUG), F32),
            mem((n_seq, HEADS // n_seq * AUG, AUG), F32),
            mem((block, n_tm * wide), BF16),
            mem((n_seq, block, n_tm * wide), BF16),
            mem((width if rows % 16 == 0 else n_tm * wide, n_seq * block), BF16),
            mem((width, 128), F32),
            mem((ch, tok), F32),
            mem((ITERS, n_seq, ch, tok), F32),
            mem((ITERS, n_tm, ch, tok), F32),
            mem((ITERS, ch, tok), F32),
            mem((ITERS, ch, tok), F32),
            mem((n_seq * block, 2 * tok), BF16),
        ] + pairs,
        compiler_params=pltpu.CompilerParams(
            collective_id=0, has_side_effects=True, vmem_limit_bytes=40 << 20
        ),
    )(z0, coef, patch_t, final_t, terms, bias, mid, qkv, wo)


def plan_coefs(beta_table, cur_ids, next_ids):
    keep = 1.0 - beta_table
    pos = jnp.arange(beta_table.shape[0], dtype=jnp.int32)
    bar_now = jnp.prod(jnp.where(pos[None] <= cur_ids[:, None], keep[None], 1.0), axis=1)
    bar_next = jnp.prod(jnp.where(pos[None] <= next_ids[:, None], keep[None], 1.0), axis=1)
    coef_a = jnp.sqrt(bar_next / bar_now)
    coef_b = jnp.sqrt(1.0 - bar_next) - coef_a * jnp.sqrt(1.0 - bar_now)
    return (coef_a, coef_b)


def frequency_embed(cur_ids, freq_width):
    half = freq_width // 2
    freqs = jnp.exp(-math.log(10000.0) * jnp.arange(half, dtype=F32) / half)
    angles = cur_ids.astype(F32)[:, None] * freqs[None, :]
    return jnp.concatenate([jnp.cos(angles), jnp.sin(angles)], axis=1)


def body(
    init_latent, cur_ids, next_ids, beta_table, temb_weight, mod_weight, mod_bias,
    patch_weight, qkv_weight, out_weight, final_weight,
):
    ch, width = patch_weight.shape
    tok = init_latent.shape[1]
    here, when = lax.axis_index("seq"), lax.axis_index("tm")
    cols = qkv_weight.shape[2]
    rows = qkv_weight.shape[0]

    coef_a, coef_b = plan_coefs(beta_table, cur_ids, next_ids)
    coef = jnp.broadcast_to(
        jnp.stack([coef_a[0] - 1.0, coef_b[0]])[:, None, None], (2, ch, tok)
    )
    freq_emb = frequency_embed(cur_ids, temb_weight.shape[0]).astype(BF16)
    feats = mod_weight.shape[0]
    temb_here = lax.dynamic_slice_in_dim(temb_weight, here * feats, feats, 1)
    emb_part = jax.nn.silu(jnp.dot(freq_emb, temb_here, preferred_element_type=F32)).astype(BF16)
    mod_terms = jnp.einsum("d,dme->me", emb_part[0], mod_weight, preferred_element_type=F32)
    spare = ((0, 8 - mod_terms.shape[0]), (0, 0))
    patch_mid = patch_weight - jnp.mean(patch_weight, axis=1, keepdims=True)
    mid_here = lax.dynamic_slice_in_dim(patch_mid, when * rows, rows, 1)
    traj, noise = picard(
        width // HEADS, init_latent, coef, patch_weight.T, final_weight.T,
        jnp.pad(mod_terms, spare), jnp.pad(mod_bias, spare), mid_here,
        jnp.swapaxes(qkv_weight, 0, 1),
        lax.dynamic_slice_in_dim(out_weight, here * cols, cols, 0),
    )
    return (traj[None], noise[None])


def solution(mesh):
    in_specs = (
        P("groups", "seq"),
        P("tm"),
        P("tm"),
        P(),
        P(),
        P("seq", None, None),
        P(),
        P(),
        P("tm", None, "seq"),
        P(None, "tm"),
        P(),
    )
    out_specs = (P("tm", "groups", "seq"), P("tm", "groups", "seq"))
    return jax.shard_map(body, mesh=mesh, in_specs=in_specs, out_specs=out_specs, check_vma=False)
```

time: 130 us -> 108 us (0.83)
  blocking collectives: 21 us -> 0 us
  Pallas kernels: 70.9 us -> 83.6 us
  other arithmetic: 10.1 us -> 3.99 us
  local copies, waits for them, and re-layouts: 16.8 us -> 13.2 us
  matrix products: 5.25 us -> 1.79 us
    all_gather x1 -> x0, blocking collectives: 21 us -> none  [body(): out_here = lax.all_gather(out_rows, 'tm', axis=1, tiled=True)]
    pallas_call x5 -> x1, Pallas kernels: 70.9 us -> 83.6 us  [picard(): pl.pallas_call(functools.partial(picard_kernel, n_seq, n_tm, head_dim), o...]
    reduce_sum x3 -> x0, other arithmetic: 4.33 us -> none  [the longest x1 2.09 us: wide_dot(): return jnp.sum(out.reshape((3, left.shape[0], right.shape[1])), axis=0)]
    dot_general x3 -> x0, matrix products: 3.35 us -> none  [the longest x2 3.12 us: wide_dot(): jnp.dot(jnp.concatenate(parts, axis=0), right, preferred_element_type=F32)]
    reshape x2 -> x0, local copies, waits for them, and re-layouts: 2.69 us -> none  [the longest x1 1.66 us: body(): jnp.einsum('che,hg->hcge', m_value[:ch], same)]
    convert_element_type x3 -> x0, other arithmetic: 2.04 us -> none  [the longest x2 1.03 us: wide_dot(): parts.append(part.astype(BF16))]
    unnamed x27 -> x22, local copies, waits for them, and re-layouts: 11.6 us -> 10.1 us
    sub x1, other arithmetic: 0.08 us -> 1.44 us  [body(): patch_mid = patch_weight - jnp.mean(patch_weight, axis=1, keepdims=True)]
where the time goes in v2:
time: 108 us
  Pallas kernels  83.6 us (77%)
  local copies, waits for them, and re-layouts  13.2 us (12%)
  between operations  5.08 us (5%)
  other arithmetic  3.99 us (4%)
  matrix products  1.79 us (2%)
    pallas_call x1, Pallas kernels, picard(): pl.pallas_call(functools.partial(picard_kernel, n_seq, n_tm, head_dim), o...  83.6 us
    unnamed x22, local copies, waits for them, and re-layouts  10.1 us

profile of v2, /device:TPU:0, one launch (start us, length us, event | category | flops | bytes accessed | tf_op | source)
XLA Modules:
  0.0 107.7 jit_solution(3725641741042403479)
XLA Ops:
  0.6 0.0 copy-start
  0.6 0.0 copy-start.8
  2.3 1.4 %select_reduce_fusion = (f32[]{:T(128)}, f32[]{:T(128)}) fusion(f32[1000]{0:T(1024)} %param.14, s32[]{:T(128)} %bitcast.16, s32[]{:T(128)} %bitcast.17), kind=kLoop, calls=%fused_computation.4 | loop fusion | flops 6998 | bytes 4016 | tf_op jit(solution)/shard_map/reduce_prod | solution.py:336
  6.4 0.1 pad_maximum_fusion
  6.5 1.0 reduce_sum.9
  7.6 1.2 %convolution_reduce_fusion = f32[288]{0:T(512)S(1)} fusion(bf16[256,1]{0,1:T(2,128)(2,1)S(1)} %reshape.64, bf16[256,1152]{1,0:T(8,128)(2,1)} %param.15, s32[]{:T(128)S(6)} %select_n.18), kind=kOutput, calls=%fused_computation | convolution fusion | flops 147456 | bytes 198276 | tf_op jit(solution)/shard_map/dot_general | solution.py:367
  8.8 0.1 broadcast_in_dim.9.coef_ref
  8.9 0.0 copy-done
  8.9 0.6 fusion.3
  9.5 0.6 pad.7.terms_ref
  10.1 1.4 %dynamic-slice_subtract_fusion.mid_ref = f32[16,288]{1,0:T(8,128)} fusion(f32[16,1152]{1,0:T(8,128)} %param.18, s32[]{:T(128)S(6)} %select_n.19, f32[16]{0:T(128)S(1)} %broadcast_multiply_fusion), kind=kLoop, calls=%fused_computation.3 | loop fusion | flops 4608 | bytes 36932 | tf_op jit(solution)/shard_map/sub | solution.py:370
  11.6 0.0 copy-done.8
  11.6 0.6 pad.8.bias_ref
  12.2 1.8 %constant_dynamic-slice_fusion = bf16[288,288]{0,1:T(8,128)(2,1)} fusion(bf16[1152,288]{0,1:T(8,128)(2,1)} %param.20, s32[]{:T(128)S(6)} %select_n.18), kind=kLoop, calls=%fused_computation.10 | loop fusion | bytes 331780 | tf_op jit(solution)/shard_map/dynamic_slice | solution.py:376
  13.9 1.1 %copy.16.wo_ref = bf16[288,288]{1,0:T(8,128)(2,1)S(1)} copy(bf16[288,288]{0,1:T(8,128)(2,1)} %constant_dynamic-slice_fusion) | data formatting | bytes 331776
  15.0 1.9 %copy.13 = f32[16,1152]{0,1:T(8,128)} copy(f32[16,1152]{1,0:T(8,128)} %param.18) | data formatting | bytes 147456 | tf_op args[7]
  17.0 0.0 copy-start.1
  17.0 1.1 copy-done.1
  18.1 0.0 copy-start.2
  18.1 1.1 %copy-done.2 = bf16[288,3,288]{2,0,1:T(8,128)(2,1)S(1)} copy-done((bf16[288,3,288]{2,0,1:T(8,128)(2,1)S(1)}, bf16[288,3,288]{2,0,1:T(8,128)(2,1)}, u32[]{:S(2)}) %copy-start.2) | copy-done | bytes 497688
  19.1 0.0 copy-start.3
  19.1 0.8 copy-done.3
  19.9 0.0 copy-start.4
  19.9 0.8 copy-done.4
  20.7 0.0 copy-start.5
  20.7 0.7 copy-done.5
  21.4 0.0 copy-start.6
  21.4 0.8 copy-done.6
  22.2 0.0 copy-start.7
  22.2 0.7 copy-done.7
  22.9 83.6 %shard_map.122 = (f32[16,128]{1,0:T(8,128)S(1)}, f32[16,128]{1,0:T(8,128)S(1)}) custom-call(f32[16,128]{1,0:T(8,128)S(1)} %copy-done.7, f32[2,16,128]{2,1,0:T(8,128)S(1)} %broadcast_in_dim.9.coef_ref, f32[1152,16]{1,0:T(8,128)S(1)} %bitcast.18, bf16[16,1152]{1,0:T(8,128)(2,1)S(1)} %bitcast.20, f32[8,1152]{1,0:T(8,128)S(1)} %copy-done.3, ...), custom_call_target="tpu_custom_call" | custom-call | tf_op jit(solution)/shard_map/pallas_call | solution.py:302
  106.5 0.6 copy.23
  107.1 0.6 copy.24
  (7 shorter events, 0.1 us)
Async XLA Ops:
  0.6 8.3 %copy-start = (bf16[288,5,1152]{2,0,1:T(8,128)(2,1)S(1)}, bf16[288,5,1152]{2,0,1:T(8,128)(2,1)}, u32[]{:S(2)}) copy-start(bf16[288,5,1152]{2,0,1:T(8,128)(2,1)} %param.16) | copy-start | bytes 9953284
  0.6 10.9 %copy-start.8 = (f32[5,1152]{1,0:T(8,128)S(1)}, f32[5,1152]{1,0:T(8,128)}, u32[]{:S(2)}) copy-start(f32[5,1152]{1,0:T(8,128)} %param.17) | copy-start | bytes 69124
  17.0 1.1 copy-start.1
  18.1 1.1 %copy-start.2 = (bf16[288,3,288]{2,0,1:T(8,128)(2,1)S(1)}, bf16[288,3,288]{2,0,1:T(8,128)(2,1)}, u32[]{:S(2)}) copy-start(bf16[288,3,288]{2,0,1:T(8,128)(2,1)} %param.19) | copy-start | bytes 1492996
  19.1 0.8 copy-start.3
  19.9 0.8 copy-start.4
  20.7 0.7 copy-start.5
  21.4 0.8 copy-start.6
  22.2 0.7 copy-start.7

commit v3 on v2

--- a/solution.py
+++ b/solution.py
@@ -95,34 +95,78 @@
 
 
 def picard_kernel(
-    n_seq, n_tm, head_dim,
-    z0_ref, coef_ref, patch_ref, final_ref, terms_ref, bias_ref, mid_ref, qkv_ref, wo_ref,
+    n_seq, n_tm, n_groups, head_dim,
+    z0_ref, coef_ref, patch_ref, final_ref, terms_ref, bias_ref, qkv_ref, wo_ref,
     traj_ref, noise_ref,
-    wbuf, tbuf, msrc, mbuf, psrc, pbuf, asrc, abuf, bsrc, bbuf, bigt, cols,
+    patch_t, ebuf, modbuf, wbuf, tbuf, msrc, mbuf, psrc, pbuf, asrc, abuf, bsrc, bbuf, bigt, cols,
     state, ubuf, dbuf, usrc, dsrc, yrows,
     wsend, wrecv, tsend, trecv, msend, mrecv, psend, precv, asend, arecv, bsend, brecv,
-    usend, urecv, dsend, drecv,
+    ysend, yrecv, usend, urecv, dsend, drecv,
 ):
-    greet([("seq", n_seq), ("tm", n_tm)])
+    halve = n_groups == 2 and wo_ref.shape[0] % 32 == 0
+    greet([("seq", n_seq), ("tm", n_tm)] + ([("groups", n_groups)] if halve else []))
     here, when = lax.axis_index("seq"), lax.axis_index("tm")
     ch, tok = z0_ref.shape
     keys = n_seq * tok
     heads_here = HEADS // n_seq
     block = heads_here * 16 + 16
-    width = patch_ref.shape[0]
-    rows = mid_ref.shape[1]
+    width = patch_ref.shape[1]
+    rows = qkv_ref.shape[1]
+    mods = bias_ref.shape[0]
     wide = bsrc.shape[1] // n_tm
 
     terms = sends("seq", n_seq, terms_ref, tbuf, tsend, trecv)
     for copy in terms:
         copy.start()
-    outs = sends("tm", n_tm, wo_ref, wbuf, wsend, wrecv)
+    if halve:
+        half = wo_ref.shape[0] // 2
+        group = lax.axis_index("groups")
+        mine = pl.ds(pl.multiple_of(group * half, 16), half)
+        outs = [
+            pltpu.make_async_remote_copy(
+                src_ref=wo_ref.at[mine], dst_ref=wbuf.at[when, mine],
+                send_sem=wsend.at[d - 1], recv_sem=wrecv.at[d - 1],
+                device_id={"tm": lax.rem(when + d, n_tm)}, device_id_type=MESH,
+            )
+            for d in range(1, n_tm)
+        ]
+    else:
+        outs = sends("tm", n_tm, wo_ref, wbuf, wsend, wrecv)
     for copy in outs:
         copy.start()
     tbuf[here] = terms_ref[...]
     wbuf[when] = wo_ref[...]
     state[...] = z0_ref[...]
     bsrc[...] = jnp.zeros_like(bsrc)
+    patch = patch_ref[...]
+    patch_t[...] = jnp.transpose(
+        jnp.concatenate([patch, jnp.zeros((128 - ch, width), F32)], axis=0)
+    )[:, :ch]
+
+    def seq_copies(it):
+        return sends("seq", n_seq, usrc.at[it], ubuf.at[it], usend.at[it], urecv.at[it])
+
+    def begin(it):
+        z = state[...]
+        emb = lax.dot_general(
+            patch_t[...], z, (((1,), (0,)), ((), ())),
+            precision=HIGH, preferred_element_type=F32,
+        )
+        center = emb - jnp.mean(emb, axis=0, keepdims=True)
+        spread = jnp.mean(center * center, axis=0, keepdims=True)
+        u = z / jnp.sqrt(spread + 1e-06)
+        usrc[it] = u
+        for copy in seq_copies(it):
+            copy.start()
+        ubuf[it, here] = u
+        ebuf[...] = emb
+
+    begin(0)
+    modbuf[...] = jnp.zeros_like(modbuf)
+    patch_mid = patch - jnp.mean(patch, axis=1, keepdims=True)
+    mid = patch_mid[:, :rows]
+    for k in range(1, n_tm):
+        mid = jnp.where(when == k, patch_mid[:, k * rows : (k + 1) * rows], mid)
 
     def ones_tail(lanes):
         row = lax.broadcasted_iota(jnp.int32, (AUG - ch, lanes), 0)
@@ -146,7 +190,8 @@
     for copy in steps:
         copy.start()
     mbuf[when] = msrc[when]
-    cols[...] = jnp.transpose(jnp.concatenate([mod, jnp.zeros((120, width), F32)], axis=0))
+    modbuf[0:mods, :] = mod
+    cols[...] = jnp.transpose(modbuf[...])
     for copy in steps:
         copy.wait()
 
@@ -154,24 +199,37 @@
     left = []
     for t in range(n_tm):
         step = mbuf[t]
-        left.append(mid_ref[...] * (1.0 + step[1:2]))
+        left.append(mid * (1.0 + step[1:2]))
         left.append(jnp.where(first, step[0:1], 0.0))
     left = split3(jnp.concatenate(left, axis=0))
-    for j in range(3):
-        part = thirds(jnp.dot(left, qkv_ref[j], preferred_element_type=F32))
-        for t in range(n_tm):
-            psrc[t, j] = part[t * AUG : (t + 1) * AUG]
+    three = [thirds(jnp.dot(left, qkv_ref[j], preferred_element_type=F32)) for j in range(3)]
+    rest = jnp.zeros((psrc.shape[1] - 3 * AUG, psrc.shape[2]), F32)
+    for t in range(n_tm):
+        piece = [part[t * AUG : (t + 1) * AUG] for part in three]
+        psrc[t] = jnp.concatenate(piece + [rest], axis=0).astype(BF16)
     parts = sends("tm", n_tm, psrc, pbuf, psend, precv, True)
     for copy in parts:
         copy.start()
     pbuf[when] = psrc[when]
+    swaps = []
+    if halve:
+        for d in range(1, n_tm):
+            outs[d - 1].wait_recv()
+            came = wbuf.at[lax.rem(when + n_tm - d, n_tm), mine]
+            swaps.append(
+                pltpu.make_async_remote_copy(
+                    src_ref=came, dst_ref=came,
+                    send_sem=ysend.at[d - 1], recv_sem=yrecv.at[d - 1],
+                    device_id={"groups": 1 - group}, device_id_type=MESH,
+                )
+            )
+            swaps[-1].start()
     for copy in parts:
         copy.wait()
-    m_query, m_key, m_value = pbuf[0, 0], pbuf[0, 1], pbuf[0, 2]
+    m_all = pbuf[0].astype(F32)
     for t in range(1, n_tm):
-        m_query, m_key, m_value = (
-            m_query + pbuf[t, 0], m_key + pbuf[t, 1], m_value + pbuf[t, 2]
-        )
+        m_all = m_all + pbuf[t].astype(F32)
+    m_query, m_key, m_value = m_all[:AUG], m_all[AUG : 2 * AUG], m_all[2 * AUG : 3 * AUG]
     spot = lax.broadcasted_iota(jnp.int32, m_key.shape, 1)
 
     def own(value, h):
@@ -191,6 +249,11 @@
     diag += [m_value[ch:], jnp.zeros((16 - AUG + ch, m_value.shape[1]), F32)]
     diag = split3(jnp.concatenate(diag, axis=0))
     for copy in outs:
+        if halve:
+            copy.wait_send()
+        else:
+            copy.wait()
+    for copy in swaps:
         copy.wait()
     for k in range(n_tm):
         bsrc[:, k * wide : k * wide + rows] = thirds(
@@ -211,18 +274,9 @@
 
     def one(it, carry):
         z = state[...]
-        emb = lax.dot_general(
-            patch_ref[...], z, (((1,), (0,)), ((), ())),
-            precision=HIGH, preferred_element_type=F32,
-        )
-        center = emb - jnp.mean(emb, axis=0, keepdims=True)
-        spread = jnp.mean(center * center, axis=0, keepdims=True)
-        u = z / jnp.sqrt(spread + 1e-06)
-        usrc[it] = u
-        copies = sends("seq", n_seq, usrc.at[it], ubuf.at[it], usend.at[it], urecv.at[it])
-        for copy in copies:
-            copy.start()
-        ubuf[it, here] = u
+        emb = ebuf[...]
+        u = usrc[it]
+        copies = seq_copies(it)
         u_query = jnp.concatenate([u, ones_tail(tok)], axis=0)
         g = lax.dot_general(
             a_all, u_query, (((1,), (0,)), ((), ())),
@@ -279,38 +333,48 @@
         for j in range(n_tm - 1):
             total = total + jnp.where(when > j, dbuf[it, j], 0.0)
         state[...] = z0_ref[...] + total
+
+        @pl.when(it < ITERS - 1)
+        def _():
+            begin(it + 1)
+
         return carry
 
     lax.fori_loop(0, ITERS, one, 0)
     traj_ref[...] = state[...]
 
 
-def picard(head_dim, z0, coef, patch_t, final_t, terms, bias, mid, qkv, wo):
+def picard(head_dim, z0, coef, patch, final_t, terms, bias, qkv, wo):
     n_seq, n_tm = lax.axis_size("seq"), lax.axis_size("tm")
     ch, tok = z0.shape
-    width = patch_t.shape[0]
-    rows, here = mid.shape[1], wo.shape[0]
+    width = patch.shape[1]
+    rows, here = qkv.shape[1], wo.shape[0]
+    mods = bias.shape[0]
+    part_rows = -(-3 * AUG // 16) * 16
     block = HEADS // n_seq * 16 + 16
     wide = -(-rows // 128) * 128
     vmem = pl.BlockSpec(memory_space=pltpu.VMEM)
     sem, mem = pltpu.SemaphoreType.DMA, pltpu.VMEM
     pairs = []
-    for n in (n_tm, n_seq, n_tm, n_tm, n_seq, n_seq):
+    for n in (n_tm, n_seq, n_tm, n_tm, n_seq, n_seq, n_tm):
         pairs += [sem((n - 1,)), sem((n - 1,))]
     for n in (n_seq, n_tm):
         pairs += [sem((ITERS, n - 1)), sem((ITERS, n - 1))]
     return pl.pallas_call(
-        functools.partial(picard_kernel, n_seq, n_tm, head_dim),
+        functools.partial(picard_kernel, n_seq, n_tm, lax.axis_size("groups"), head_dim),
         out_shape=[jax.ShapeDtypeStruct((ch, tok), F32)] * 2,
-        in_specs=[vmem] * 9,
+        in_specs=[vmem] * 8,
         out_specs=[vmem] * 2,
         scratch_shapes=[
+            mem((width, ch), F32),
+            mem((width, tok), F32),
+            mem((128, width), F32),
             mem((n_tm,) + wo.shape, BF16),
             mem((n_seq,) + terms.shape, F32),
-            mem((n_tm, 8, rows), F32),
-            mem((n_tm, 8, rows), F32),
-            mem((n_tm, 3, AUG, here), F32),
-            mem((n_tm, 3, AUG, here), F32),
+            mem((n_tm, mods, rows), F32),
+            mem((n_tm, mods, rows), F32),
+            mem((n_tm, part_rows, here), BF16),
+            mem((n_tm, part_rows, here), BF16),
             mem((HEADS // n_seq * AUG, AUG), F32),
             mem((n_seq, HEADS // n_seq * AUG, AUG), F32),
             mem((block, n_tm * wide), BF16),
@@ -327,7 +391,7 @@
         compiler_params=pltpu.CompilerParams(
             collective_id=0, has_side_effects=True, vmem_limit_bytes=40 << 20
         ),
-    )(z0, coef, patch_t, final_t, terms, bias, mid, qkv, wo)
+    )(z0, coef, patch, final_t, terms, bias, qkv, wo)
 
 
 def plan_coefs(beta_table, cur_ids, next_ids):
@@ -353,9 +417,8 @@
 ):
     ch, width = patch_weight.shape
     tok = init_latent.shape[1]
-    here, when = lax.axis_index("seq"), lax.axis_index("tm")
+    here = lax.axis_index("seq")
     cols = qkv_weight.shape[2]
-    rows = qkv_weight.shape[0]
 
     coef_a, coef_b = plan_coefs(beta_table, cur_ids, next_ids)
     coef = jnp.broadcast_to(
@@ -366,12 +429,8 @@
     temb_here = lax.dynamic_slice_in_dim(temb_weight, here * feats, feats, 1)
     emb_part = jax.nn.silu(jnp.dot(freq_emb, temb_here, preferred_element_type=F32)).astype(BF16)
     mod_terms = jnp.einsum("d,dme->me", emb_part[0], mod_weight, preferred_element_type=F32)
-    spare = ((0, 8 - mod_terms.shape[0]), (0, 0))
-    patch_mid = patch_weight - jnp.mean(patch_weight, axis=1, keepdims=True)
-    mid_here = lax.dynamic_slice_in_dim(patch_mid, when * rows, rows, 1)
     traj, noise = picard(
-        width // HEADS, init_latent, coef, patch_weight.T, final_weight.T,
-        jnp.pad(mod_terms, spare), jnp.pad(mod_bias, spare), mid_here,
+        width // HEADS, init_latent, coef, patch_weight, final_weight.T, mod_terms, mod_bias,
         jnp.swapaxes(qkv_weight, 0, 1),
         lax.dynamic_slice_in_dim(out_weight, here * cols, cols, 0),
     )

time: 108 us -> 84.1 us (0.78)
  Pallas kernels: 83.6 us -> 65.4 us
  local copies, waits for them, and re-layouts: 13.2 us -> 9.75 us
  other arithmetic: 3.99 us -> 1.53 us
    pallas_call x1, Pallas kernels: 83.6 us -> 65.4 us  [picard(): pl.pallas_call(functools.partial(picard_kernel, n_seq, n_tm, lax.axis_siz...]
    unnamed x22 -> x17, local copies, waits for them, and re-layouts: 10.1 us -> 7.28 us
    sub x1 -> x0, other arithmetic: 1.44 us -> none  [body(): patch_mid = patch_weight - jnp.mean(patch_weight, axis=1, keepdims=True)]
    pad x2 -> x0, local copies, waits for them, and re-layouts: 1.23 us -> none  [the longest x1 0.63 us: body(): jnp.pad(mod_terms, spare)]
where the time goes in v3:
time: 84.1 us; the launch traced here: 83.5 us
  Pallas kernels  65.4 us (78%)
  local copies, waits for them, and re-layouts  9.75 us (12%)
  between operations  4.96 us (6%)
  matrix products  1.79 us (2%)
  other arithmetic  1.53 us (2%)
    pallas_call x1, Pallas kernels, picard(): pl.pallas_call(functools.partial(picard_kernel, n_seq, n_tm, lax.axis_siz...  65.4 us
    unnamed x17, local copies, waits for them, and re-layouts  7.28 us
    dynamic_slice x1, local copies, waits for them, and re-layouts, body(): lax.dynamic_slice_in_dim(out_weight, here * cols, cols, 0)  1.76 us

profile of v3, /device:TPU:0, one launch (start us, length us, event | category | flops | bytes accessed | tf_op | source)
XLA Modules:
  0.0 83.5 jit_solution(5745406478421502078)
XLA Ops:
  0.6 0.0 copy-start
  2.3 1.4 %select_reduce_fusion = (f32[]{:T(128)}, f32[]{:T(128)}) fusion(f32[1000]{0:T(1024)} %param.14, s32[]{:T(128)} %bitcast.15, s32[]{:T(128)} %bitcast.16), kind=kLoop, calls=%fused_computation.3 | loop fusion | flops 6998 | bytes 4016 | tf_op jit(solution)/shard_map/reduce_prod | solution.py:400
  6.3 0.1 pad_maximum_fusion
  6.4 1.2 %convolution_reduce_fusion = f32[288]{0:T(512)S(1)} fusion(bf16[256,1]{0,1:T(2,128)(2,1)S(1)} %reshape.60, bf16[256,1152]{1,0:T(8,128)(2,1)} %param.15, s32[]{:T(128)S(6)} %select_n.15), kind=kOutput, calls=%fused_computation | convolution fusion | flops 147456 | bytes 198276 | tf_op jit(solution)/shard_map/dot_general | solution.py:430
  7.7 0.1 broadcast_in_dim.9.coef_ref
  7.8 0.0 copy-done
  7.8 0.6 fusion.3
  8.3 0.6 copy.17
  9.0 1.8 %constant_dynamic-slice_fusion = bf16[288,288]{0,1:T(8,128)(2,1)} fusion(bf16[1152,288]{0,1:T(8,128)(2,1)} %param.20, s32[]{:T(128)S(6)} %select_n.15), kind=kLoop, calls=%fused_computation.11 | loop fusion | bytes 331780 | tf_op jit(solution)/shard_map/dynamic_slice | solution.py:435
  10.7 1.1 %copy.15.wo_ref = bf16[288,288]{1,0:T(8,128)(2,1)S(1)} copy(bf16[288,288]{0,1:T(8,128)(2,1)} %constant_dynamic-slice_fusion) | data formatting | bytes 331776
  11.8 0.0 copy-start.1
  11.9 1.1 %copy-done.1 = bf16[288,3,288]{2,0,1:T(8,128)(2,1)S(1)} copy-done((bf16[288,3,288]{2,0,1:T(8,128)(2,1)S(1)}, bf16[288,3,288]{2,0,1:T(8,128)(2,1)}, u32[]{:S(2)}) %copy-start.1) | copy-done | bytes 497688
  12.9 0.0 copy-start.2
  12.9 0.8 copy-done.2
  13.7 0.0 copy-start.3
  13.7 0.9 %copy-done.3 = f32[16,1152]{1,0:T(8,128)S(1)} copy-done((f32[16,1152]{1,0:T(8,128)S(1)}, f32[16,1152]{1,0:T(8,128)}, u32[]{:S(2)}) %copy-start.3) | copy-done | bytes 73752
  14.6 0.0 copy-start.4
  14.6 0.8 copy-done.4
  15.4 0.0 copy-start.5
  15.4 0.8 copy-done.5
  16.1 0.0 copy-start.6
  16.1 0.7 copy-done.6
  16.8 65.4 %shard_map.122 = (f32[16,128]{1,0:T(8,128)S(1)}, f32[16,128]{1,0:T(8,128)S(1)}) custom-call(f32[16,128]{1,0:T(8,128)S(1)} %copy-done.6, f32[2,16,128]{2,1,0:T(8,128)S(1)} %broadcast_in_dim.9.coef_ref, f32[16,1152]{1,0:T(8,128)S(1)} %copy-done.3, bf16[16,1152]{1,0:T(8,128)(2,1)S(1)} %bitcast.19, f32[5,1152]{1,0:T(8,128)S(1)} %bitcast.18, ...), custom_call_target="tpu_custom_call" | custom-call | tf_op jit(solution)/shard_map/pallas_call | solution.py:363
  82.3 0.6 copy.22
  82.9 0.6 copy.23
  (5 shorter events, 0.1 us)
Async XLA Ops:
  0.6 7.1 %copy-start = (bf16[288,5,1152]{2,0,1:T(8,128)(2,1)S(1)}, bf16[288,5,1152]{2,0,1:T(8,128)(2,1)}, u32[]{:S(2)}) copy-start(bf16[288,5,1152]{2,0,1:T(8,128)(2,1)} %param.16) | copy-start | bytes 9953284
  11.8 1.1 %copy-start.1 = (bf16[288,3,288]{2,0,1:T(8,128)(2,1)S(1)}, bf16[288,3,288]{2,0,1:T(8,128)(2,1)}, u32[]{:S(2)}) copy-start(bf16[288,3,288]{2,0,1:T(8,128)(2,1)} %param.19) | copy-start | bytes 1492996
  12.9 0.8 copy-start.2
  13.7 0.9 %copy-start.3 = (f32[16,1152]{1,0:T(8,128)S(1)}, f32[16,1152]{1,0:T(8,128)}, u32[]{:S(2)}) copy-start(f32[16,1152]{1,0:T(8,128)} %patch_ref.1) | copy-start | bytes 221188
  14.6 0.8 copy-start.4
  15.4 0.8 copy-start.5
  16.1 0.7 copy-start.6

commit v4 on v3

--- a/solution.py
+++ b/solution.py
@@ -94,8 +94,16 @@
     onward.wait()
 
 
+def load_kernel(n_seq, n_tm, n_groups, head_dim, count, *refs):
+    held, sems = refs[-count - 1 : -1], refs[-1]
+    loads = [pltpu.make_async_copy(refs[i], held[i], sems.at[i]) for i in range(count)]
+    for load in loads:
+        load.start()
+    picard_kernel(loads, n_seq, n_tm, n_groups, head_dim, *held, *refs[count : -count - 1])
+
+
 def picard_kernel(
-    n_seq, n_tm, n_groups, head_dim,
+    loads, n_seq, n_tm, n_groups, head_dim,
     z0_ref, coef_ref, patch_ref, final_ref, terms_ref, bias_ref, qkv_ref, wo_ref,
     traj_ref, noise_ref,
     patch_t, ebuf, modbuf, wbuf, tbuf, msrc, mbuf, psrc, pbuf, asrc, abuf, bsrc, bbuf, bigt, cols,
@@ -105,6 +113,8 @@
 ):
     halve = n_groups == 2 and wo_ref.shape[0] % 32 == 0
     greet([("seq", n_seq), ("tm", n_tm)] + ([("groups", n_groups)] if halve else []))
+    for load in loads:
+        load.wait()
     here, when = lax.axis_index("seq"), lax.axis_index("tm")
     ch, tok = z0_ref.shape
     keys = n_seq * tok
@@ -350,6 +360,7 @@
     width = patch.shape[1]
     rows, here = qkv.shape[1], wo.shape[0]
     mods = bias.shape[0]
+    values = (z0, coef, patch, final_t, terms, bias, qkv, wo)
     part_rows = -(-3 * AUG // 16) * 16
     block = HEADS // n_seq * 16 + 16
     wide = -(-rows // 128) * 128
@@ -361,9 +372,11 @@
     for n in (n_seq, n_tm):
         pairs += [sem((ITERS, n - 1)), sem((ITERS, n - 1))]
     return pl.pallas_call(
-        functools.partial(picard_kernel, n_seq, n_tm, lax.axis_size("groups"), head_dim),
+        functools.partial(
+            load_kernel, n_seq, n_tm, lax.axis_size("groups"), head_dim, len(values)
+        ),
         out_shape=[jax.ShapeDtypeStruct((ch, tok), F32)] * 2,
-        in_specs=[vmem] * 8,
+        in_specs=[pl.BlockSpec(memory_space=pl.ANY)] * len(values),
         out_specs=[vmem] * 2,
         scratch_shapes=[
             mem((width, ch), F32),
@@ -387,11 +400,11 @@
             mem((ITERS, ch, tok), F32),
             mem((ITERS, ch, tok), F32),
             mem((n_seq * block, 2 * tok), BF16),
-        ] + pairs,
+        ] + pairs + [mem(v.shape, v.dtype) for v in values] + [sem((len(values),))],
         compiler_params=pltpu.CompilerParams(
-            collective_id=0, has_side_effects=True, vmem_limit_bytes=40 << 20
+            collective_id=0, has_side_effects=True, vmem_limit_bytes=56 << 20
         ),
-    )(z0, coef, patch, final_t, terms, bias, qkv, wo)
+    )(*values)
 
 
 def plan_coefs(beta_table, cur_ids, next_ids):

time: 84.1 us -> 80.5 us (0.957)
  local copies, waits for them, and re-layouts: 9.75 us -> 5.83 us
    unnamed x17 -> x5, local copies, waits for them, and re-layouts: 7.28 us -> 3.43 us
where the time goes in v4:
time: 80.5 us; the launch traced here: 80.1 us
  Pallas kernels  66.2 us (82%)
  local copies, waits for them, and re-layouts  5.83 us (7%)
  between operations  4.86 us (6%)
  matrix products  1.78 us (2%)
  other arithmetic  1.5 us (2%)
    pallas_call x1, Pallas kernels, picard(): pl.pallas_call(functools.partial(load_kernel, n_seq, n_tm, lax.axis_size(...  66.2 us
    unnamed x5, local copies, waits for them, and re-layouts  3.43 us

profile of v4, /device:TPU:0, one launch (start us, length us, event | category | flops | bytes accessed | tf_op | source)
XLA Modules:
  0.0 80.1 jit_solution(18381047054499566699)
XLA Ops:
  0.6 0.0 copy-start
  2.3 1.4 %select_reduce_fusion = (f32[]{:T(128)}, f32[]{:T(128)}) fusion(f32[1000]{0:T(1024)} %param.14, s32[]{:T(128)} %bitcast.15, s32[]{:T(128)} %bitcast.16), kind=kLoop, calls=%fused_computation.3 | loop fusion | flops 6998 | bytes 4016 | tf_op jit(solution)/shard_map/reduce_prod | solution.py:413
  6.2 0.1 pad_maximum_fusion
  6.3 1.2 %convolution_reduce_fusion = f32[288]{0:T(512)S(1)} fusion(bf16[256,1]{0,1:T(2,128)(2,1)S(1)} %reshape.60, bf16[256,1152]{1,0:T(8,128)(2,1)} %param.15, s32[]{:T(128)S(6)} %select_n.15), kind=kOutput, calls=%fused_computation | convolution fusion | flops 147456 | bytes 198276 | tf_op jit(solution)/shard_map/dot_general | solution.py:443
  7.6 0.7 broadcast_in_dim.9.refs_1_
  8.2 0.0 copy-done
  8.2 0.6 fusion.3
  8.8 0.6 copy.17
  9.4 1.1 %constant_dynamic-slice_fusion = bf16[288,288]{0,1:T(8,128)(2,1)S(1)} fusion(bf16[1152,288]{0,1:T(8,128)(2,1)} %param.20, s32[]{:T(128)S(6)} %select_n.15), kind=kLoop, calls=%fused_computation.11 | loop fusion | bytes 331780 | tf_op jit(solution)/shard_map/dynamic_slice | solution.py:448
  10.5 0.8 %copy.15.refs_7_ = bf16[288,288]{1,0:T(8,128)(2,1)} copy(bf16[288,288]{0,1:T(8,128)(2,1)S(1)} %constant_dynamic-slice_fusion) | data formatting | bytes 331776
  11.4 66.2 %shard_map.122 = (f32[16,128]{1,0:T(8,128)}, f32[16,128]{1,0:T(8,128)}) custom-call(f32[16,128]{1,0:T(8,128)} %refs_0_.1, f32[2,16,128]{2,1,0:T(8,128)} %broadcast_in_dim.9.refs_1_, f32[16,1152]{1,0:T(8,128)} %refs_2_.1, bf16[16,1152]{1,0:T(8,128)(2,1)} %bitcast.19, f32[5,1152]{1,0:T(8,128)} %bitcast.18, f32[5,1152]{1,0:T(8,128)} %refs_5_.1, ...), custom_call_target="tpu_custom_call" | custom-call | tf_op jit(solution)/shard_map/pallas_call | solution.py:374
  77.5 1.3 %copy.22 = f32[1,16,128]{2,1,0:T(8,128)} copy(f32[1,16,128]{2,1,0:T(8,128)} %bitcast.21) | data formatting | bytes 16384
  78.8 1.3 %copy.23 = f32[1,16,128]{2,1,0:T(8,128)} copy(f32[1,16,128]{2,1,0:T(8,128)} %bitcast.20) | data formatting | bytes 16384
  (5 shorter events, 0.1 us)
Async XLA Ops:
  0.6 7.6 %copy-start = (bf16[288,5,1152]{2,0,1:T(8,128)(2,1)S(1)}, bf16[288,5,1152]{2,0,1:T(8,128)(2,1)}, u32[]{:S(2)}) copy-start(bf16[288,5,1152]{2,0,1:T(8,128)(2,1)} %param.16) | copy-start | bytes 9953284
